TPU v7x, 32 devices: a whole 2x2x4 slice. The times are simulated.
32 devices in a mesh: groups: 2 (over x), wide: 16 (over z, y, core).
Axes of the slice: x: 2, y: 2, z: 4, core: 2. Of those that a mesh axis runs over, the one named last changes fastest.
Arguments:
- prefill_blocks: bfloat16 [2048, 128, 576], P(('groups', 'wide')), parts along dimension 0, may hold values from -8 to 8
- block_owner: int32 [2048], P(('groups', 'wide')), parts along dimension 0, may hold values from -1 to 15, as said below
- block_position: int32 [2048], P(('groups', 'wide')), parts along dimension 0, may hold values from 0 to 63, as said below
- cache_len: int32 [32], P(('groups', 'wide')), parts along dimension 0, may hold values from 1 to 8192, as said below
- query_nope: bfloat16 [32, 3, 128, 128], P('groups', None, 'wide'), parts along dimension 0, may hold values from -6 to 6
- query_rope: bfloat16 [32, 3, 128, 64], P('groups', None, 'wide'), parts along dimension 0, may hold values from -256 to 256
- w_uk: bfloat16 [128, 128, 512], P('wide'), may hold values from -0.5 to 0.5
- w_uv: bfloat16 [128, 512, 128], P('wide'), may hold values from -2 to 2
- w_o: bfloat16 [16384, 7168], P('wide'), may hold values from -0.046875 to 0.046875
- new_latent: bfloat16 [32, 3, 576], P(('groups', 'wide')), parts along dimension 0, may hold values from -6 to 6
Outputs:
- layer_out: bfloat16 [32, 3, 7168], P(('groups', 'wide')), parts along dimension 0
There are 2 independent parts, one for each index of `groups`. A program takes and returns all parts, laid end to end along the dimension named above; an argument that names none is the same for every part. Nothing has to cross between parts.
Inputs may be any that keep to these rules, and one draw needn't show every extreme that they name: `block_owner`: device i of wide owns request i. No device sends more than 4 blocks to one owner, and some device sends exactly 4 to some owner. Owner r receives 64 // 2 to 64 blocks (at least 1), with block_position 0 up to their count less one, each once; some owner receives 64. `block_position`: 0 on empty slots. `cache_len`: all blocks of a request but its last are full; the last holds 1 to 128 live tokens.
All inputs are finite; a program needn't handle non-finite values.
Results may differ from a plain program's by a relative error of at most 0.0095.
Values may be sent and summed in bfloat16 or wider, within the bound.
A program may use at most 128 MiB of HBM per device.

v0:
```python
import math

import jax
import jax.numpy as jnp
from jax import lax
from jax.sharding import PartitionSpec as P


def per_device(
    prefill_blocks,
    block_owner,
    block_position,
    cache_len,
    query_nope,
    query_rope,
    w_uk,
    w_uv,
    w_o,
    new_latent,
):
    members = lax.axis_size("wide")
    local_slots = prefill_blocks.shape[0]
    block_tok = prefill_blocks.shape[1]
    key_width = prefill_blocks.shape[2]
    latent = w_uk.shape[2]
    per_peer = (local_slots + members - 1) // members
    channels = members * per_peer
    is_live = block_owner >= 0
    target = jnp.where(is_live, block_owner, members)
    slot_order = jnp.arange(local_slots)
    same_peer = (target[:, None] == target[None, :]) & (slot_order[None, :] < slot_order[:, None])
    peer_rank = jnp.sum(same_peer.astype(jnp.int32), axis=1)
    slot_of = jnp.where(is_live, target * per_peer + peer_rank, channels)
    matches = slot_of[None, :] == jnp.arange(channels)[:, None]
    source_row = jnp.sum(jnp.where(matches, slot_order[None, :], 0), axis=1)
    filled = jnp.any(matches, axis=1)
    outgoing = jnp.where(
        filled[:, None, None], prefill_blocks[source_row], jnp.zeros((), prefill_blocks.dtype)
    )
    tag_values = jnp.where(filled, block_position[source_row] + 1, 0).astype(jnp.bfloat16)
    q_latent = jnp.einsum(
        "rshn,hnc->rshc", query_nope, w_uk, preferred_element_type=jnp.float32
    ).astype(jnp.bfloat16)
    query_full = jnp.concatenate([q_latent, query_rope], axis=3)
    step_count = query_full.shape[1]
    heads_here = query_full.shape[2]
    heads_all = members * heads_here
    incoming, arrived = (
        lax.all_to_all(outgoing, "wide", split_axis=0, concat_axis=0, tiled=True),
        lax.all_to_all(tag_values, "wide", split_axis=0, concat_axis=0, tiled=True),
    )
    gathered = lax.all_to_all(query_full, "wide", split_axis=0, concat_axis=2, tiled=True)
    query_rows = gathered.reshape(step_count * heads_all, key_width)
    my_len = cache_len[0]
    position = arrived.astype(jnp.int32)
    tokens = jnp.arange(block_tok)
    is_valid = (position[:, None] > 0) & (
        (position[:, None] - 1) * block_tok + tokens[None, :] < my_len
    )
    score_scale = (query_nope.shape[3] + query_rope.shape[3]) ** (-0.5)
    flat_keys = incoming.reshape(-1, key_width)
    flat_valid = is_valid.reshape(-1)
    block_rows = math.gcd(flat_keys.shape[0], 1024)
    key_blocks = flat_keys.reshape(-1, block_rows, key_width)
    valid_blocks = flat_valid.reshape(-1, block_rows)
    total_rows = query_rows.shape[0]

    def absorb(carry, key_rows, key_mask):
        running_max, weight_total, summed = carry
        scores = (
            lax.dot_general(
                query_rows, key_rows, (((1,), (1,)), ((), ())), preferred_element_type=jnp.float32
            )
            * score_scale
        )
        scores = jnp.where(key_mask, scores, -1e30)
        fresh_max = jnp.maximum(running_max, jnp.max(scores, axis=1))
        weights = jnp.where(key_mask, jnp.exp(scores - fresh_max[:, None]), 0.0)
        factor = jnp.exp(running_max - fresh_max)
        weight_total = weight_total * factor + jnp.sum(weights, axis=1)
        summed = summed * factor[:, None] + jnp.dot(
            weights.astype(jnp.bfloat16), key_rows[:, :latent], preferred_element_type=jnp.float32
        )
        return (fresh_max, weight_total, summed)

    def scan_step(carry, inputs):
        return (absorb(carry, inputs[0], inputs[1][None, :]), None)

    start_state = (
        jnp.full((total_rows,), -1e30, jnp.float32),
        jnp.zeros((total_rows,), jnp.float32),
        jnp.zeros((total_rows, latent), jnp.float32),
    )
    state, _ = lax.scan(scan_step, start_state, (key_blocks, valid_blocks))
    fresh_keys = new_latent[0]
    causal_mask = (jnp.arange(total_rows) // heads_all)[:, None] >= jnp.arange(step_count)[None, :]
    running_max, weight_total, summed = absorb(state, fresh_keys, causal_mask)
    latent_out = (
        (summed / weight_total[:, None])
        .astype(jnp.bfloat16)
        .reshape(1, step_count, heads_all, latent)
    )
    returned = lax.all_to_all(latent_out, "wide", split_axis=2, concat_axis=0, tiled=True)
    values = jnp.einsum(
        "rshc,hcv->rshv", returned, w_uv, preferred_element_type=jnp.float32
    ).astype(jnp.bfloat16)
    values = values.reshape(members, step_count, -1)
    layer_out = lax.psum_scatter(
        jnp.einsum("rsk,kd->rsd", values, w_o, preferred_element_type=jnp.float32),
        "wide",
        scatter_dimension=0,
        tiled=True,
    )
    return layer_out.astype(jnp.bfloat16)


def solution(mesh):
    in_specs = (
        P(("groups", "wide"), None, None),
        P(("groups", "wide")),
        P(("groups", "wide")),
        P(("groups", "wide")),
        P("groups", None, "wide", None),
        P("groups", None, "wide", None),
        P("wide", None, None),
        P("wide", None, None),
        P("wide", None),
        P(("groups", "wide"), None, None),
    )
    out_specs = P(("groups", "wide"), None, None)
    return jax.shard_map(
        per_device, mesh=mesh, in_specs=in_specs, out_specs=out_specs, check_vma=False
    )
```

profile of v0, /device:TPU:0, one launch (start us, length us, event | category | flops | bytes accessed | tf_op | source)
XLA Modules:
  0.0 408.4 jit_solution(5408015807607023994)
XLA Ops:
  1.9 1.4 gather_fusion
  4.0 7.4 %all-to-all-start = ((bf16[16,4,1]{1,2,0:T(2,128)(2,1)}), bf16[16,4,1]{1,2,0:T(2,128)(2,1)S(1)}, u32[]{:S(2)}, u32[]{:S(2)}) async-start(bf16[16,4,1]{1,2,0:T(2,128)(2,1)} %convert_element_type.64), calls=%async_computation | async-start | bytes 16384 | tf_op jit(solution)/shard_map/all_to_all | solution.py:50
  12.3 1.2 fusion.13
  13.5 9.8 %gather_fusion.1 = bf16[64,128,576]{1,2,0:T(8,128)(2,1)} fusion(bf16[64,128,576]{1,2,0:T(8,128)(2,1)} %param.12, s32[1024]{0:T(1024)S(1)} %pad_clamp_fusion), kind=kCustom, calls=%fused_computation.1 | custom fusion | bytes 18874624 | tf_op jit(solution)/shard_map/gather | solution.py:38
  24.2 6.0 %all-to-all-start.2 = ((bf16[16,3,8,576]{3,2,1,0:T(8,128)(2,1)}), bf16[16,3,8,576]{3,2,1,0:T(8,128)(2,1)S(1)}, u32[]{:S(2)}, u32[]{:S(2)}) async-start(bf16[16,3,8,576]{3,2,1,0:T(8,128)(2,1)} %copy.58), calls=%async_computation.2 | async-start | bytes 983040 | tf_op jit(solution)/shard_map/all_to_all | solution.py:52
  30.2 8.0 %broadcast_select_fusion = bf16[64,128,576]{1,2,0:T(8,128)(2,1)} fusion(bf16[64,128,576]{1,2,0:T(8,128)(2,1)} %gather_fusion.1, pred[64]{0:T(512)(128)(4,1)S(1)} %fusion.24), kind=kLoop, calls=%fused_computation.21 | loop fusion | flops 4718592 | bytes 18874432 | tf_op jit(solution)/shard_map/jit(_where)/select_n | solution.py:37
  38.2 5.8 %all-to-all-done.2 = bf16[16,3,8,576]{3,2,1,0:T(8,128)(2,1)S(1)} async-done(((bf16[16,3,8,576]{3,2,1,0:T(8,128)(2,1)}), bf16[16,3,8,576]{3,2,1,0:T(8,128)(2,1)S(1)}, u32[]{:S(2)}, u32[]{:S(2)}) %all-to-all-start.2) | async-done | bytes 442400 | tf_op jit(solution)/shard_map/all_to_all | solution.py:52
  44.0 4.8 %all-to-all-start.1 = ((bf16[64,128,576]{1,2,0:T(8,128)(2,1)}), bf16[64,128,576]{1,2,0:T(8,128)(2,1)}, u32[]{:S(2)}, u32[]{:S(2)}) async-start(bf16[64,128,576]{1,2,0:T(8,128)(2,1)} %broadcast_select_fusion), calls=%async_computation.1 | async-start | bytes 18874368 | tf_op jit(solution)/shard_map/all_to_all | solution.py:49
  50.3 167.4 %all-to-all-done.1 = bf16[64,128,576]{1,2,0:T(8,128)(2,1)} async-done(((bf16[64,128,576]{1,2,0:T(8,128)(2,1)}), bf16[64,128,576]{1,2,0:T(8,128)(2,1)}, u32[]{:S(2)}, u32[]{:S(2)}) %all-to-all-start.1) | async-done | bytes 9437216 | tf_op jit(solution)/shard_map/all_to_all | solution.py:49
  217.7 14.1 %copy.55 = bf16[64,128,576]{2,1,0:T(8,128)(2,1)} copy(bf16[64,128,576]{1,2,0:T(8,128)(2,1)} %all-to-all-done.1) | data formatting | bytes 18874368 | tf_op jit(solution)/shard_map/all_to_all | solution.py:49
  231.7 37.8 %while.15 = (s32[]{:T(128)}, f32[384]{0:T(512)S(1)}, f32[384]{0:T(512)S(1)}, f32[384,512]{1,0:T(8,128)S(1)}, pred[8,1024]{1,0:T(8,128)(4,1)S(1)}, /*index=5*/bf1...) while((s32[]{:T(128)}, f32[384]{0:T(512)S(1)}, f32[384]{0:T(512)S(1)}, ...), condition=%wide.region_6.7_spmd.clone, body=%wide.region_3.6_spmd.clone.sunk | while | flops 859768704 | bytes 20789416 | solution.py:94
  231.7 1.4 dynamic-slice_bitcast_fusion.2
  236.5 1.4 dynamic-slice_bitcast_fusion.2
  241.2 1.4 dynamic-slice_bitcast_fusion.2
  245.9 1.4 dynamic-slice_bitcast_fusion.2
  250.6 1.4 dynamic-slice_bitcast_fusion.2
  255.4 1.4 dynamic-slice_bitcast_fusion.2
  260.1 1.4 dynamic-slice_bitcast_fusion.2
  264.8 1.4 dynamic-slice_bitcast_fusion.2
  269.9 1.1 copy.60
  271.1 40.7 %all-to-all-start.3 = ((bf16[1,3,128,512]{3,1,0,2:T(4,128)(2,1)}), bf16[1,3,128,512]{3,1,0,2:T(4,128)(2,1)S(1)}, u32[]{:S(2)}, u32[]{:S(2)}) async-start(bf16[1,3,128,512]{3,1,0,2:T(4,128)(2,1)} %copy.60), calls=%async_computation.3 | async-start | bytes 1048576 | tf_op jit(solution)/shard_map/all_to_all | solution.py:103
  312.3 13.9 %all-to-all-done.3 = bf16[1,3,128,512]{3,1,0,2:T(4,128)(2,1)S(1)} async-done(((bf16[1,3,128,512]{3,1,0,2:T(4,128)(2,1)}), bf16[1,3,128,512]{3,1,0,2:T(4,128)(2,1)S(1)}, u32[]{:S(2)}, u32[]{:S(2)}) %all-to-all-start.3) | async-done | bytes 393248 | tf_op jit(solution)/shard_map/all_to_all | solution.py:103
  326.7 8.0 %fusion.9 = f32[16,3,7168]{2,0,1:T(8,128)S(1)} fusion(bf16[1024,7168]{1,0:T(8,128)(2,1)} %param.20, bf16[8,3,2,8,128]{4,3,2,1,0:T(8,128)(2,1)S(1)} %fusion.14), kind=kOutput, calls=%fused_computation.19 | convolution fusion | flops 704643072 | bytes 16154624 | tf_op jit(solution)/shard_map/rsk,kd->rsd/dot_general | solution.py:109
  334.6 72.3 %all-reduce.2 = bf16[16,3,7168]{2,0,1:T(8,128)(2,1)S(1)} all-reduce(f32[16,3,7168]{2,0,1:T(8,128)S(1)} %fusion.9), channel_id=2, replica_groups=mesh['groups'=2,'wide'=16] {'wide'}, use_global_device_ids=true, to_apply=%region_9.10.clone | all-reduce | flops 344064 | bytes 2064384
  (133 shorter events, 33.9 us)
Async XLA Ops:
  0.0 12.3 %copy-start = (bf16[8,128,512]{2,1,0:T(8,128)(2,1)S(1)}, bf16[8,128,512]{2,1,0:T(8,128)(2,1)}, u32[]{:S(2)}) copy-start(bf16[8,128,512]{2,1,0:T(8,128)(2,1)} %param.18) | copy-start | bytes 3145732
  4.0 20.2 %all-to-all-start = ((bf16[16,4,1]{1,2,0:T(2,128)(2,1)}), bf16[16,4,1]{1,2,0:T(2,128)(2,1)S(1)}, u32[]{:S(2)}, u32[]{:S(2)}) async-start(bf16[16,4,1]{1,2,0:T(2,128)(2,1)} %convert_element_type.64), calls=%async_computation | async-start | bytes 16384 | tf_op jit(solution)/shard_map/all_to_all | solution.py:50
  24.2 19.8 %all-to-all-start.2 = ((bf16[16,3,8,576]{3,2,1,0:T(8,128)(2,1)}), bf16[16,3,8,576]{3,2,1,0:T(8,128)(2,1)S(1)}, u32[]{:S(2)}, u32[]{:S(2)}) async-start(bf16[16,3,8,576]{3,2,1,0:T(8,128)(2,1)} %copy.58), calls=%async_computation.2 | async-start | bytes 983040 | tf_op jit(solution)/shard_map/all_to_all | solution.py:52
  38.2 11.8 %copy-start.5 = (bf16[1,3,576]{2,1,0:T(4,128)(2,1)S(1)}, bf16[1,3,576]{2,1,0:T(4,128)(2,1)}, u32[]{:S(2)}) copy-start(bf16[1,3,576]{2,1,0:T(4,128)(2,1)} %param.21) | copy-start | bytes 10372
  44.0 173.7 %all-to-all-start.1 = ((bf16[64,128,576]{1,2,0:T(8,128)(2,1)}), bf16[64,128,576]{1,2,0:T(8,128)(2,1)}, u32[]{:S(2)}, u32[]{:S(2)}) async-start(bf16[64,128,576]{1,2,0:T(8,128)(2,1)} %broadcast_select_fusion), calls=%async_computation.1 | async-start | bytes 18874368 | tf_op jit(solution)/shard_map/all_to_all | solution.py:49
  233.2 1.1 copy-start.2
  234.3 1.3 copy-start.3
  237.9 1.1 copy-start.2
  239.0 1.3 copy-start.3
  242.6 1.1 copy-start.2
  243.7 1.3 copy-start.3
  247.4 1.1 copy-start.2
  248.4 1.3 copy-start.3
  252.1 1.1 copy-start.2
  253.2 1.3 copy-start.3
  256.8 1.1 copy-start.2
  257.9 1.3 copy-start.3
  261.5 1.1 copy-start.2
  262.6 1.3 copy-start.3
  267.3 1.3 copy-start.3
  269.9 41.8 %copy-start.6 = (u32[32]{0:T(128)S(1)}, u32[32]{0:T(128)}, u32[]{:S(2)}) copy-start(u32[32]{0:T(128)} %constant.73) | copy-start | bytes 388
  269.9 56.3 %copy-start.4 = (bf16[8,512,128]{2,1,0:T(8,128)(2,1)S(1)}, bf16[8,512,128]{2,1,0:T(8,128)(2,1)}, u32[]{:S(2)}) copy-start(bf16[8,512,128]{2,1,0:T(8,128)(2,1)} %param.19) | copy-start | bytes 3145732
  271.1 55.2 %all-to-all-start.3 = ((bf16[1,3,128,512]{3,1,0,2:T(4,128)(2,1)}), bf16[1,3,128,512]{3,1,0,2:T(4,128)(2,1)S(1)}, u32[]{:S(2)}, u32[]{:S(2)}) async-start(bf16[1,3,128,512]{3,1,0,2:T(4,128)(2,1)} %copy.60), calls=%async_computation.3 | async-start | bytes 1048576 | tf_op jit(solution)/shard_map/all_to_all | solution.py:103
  326.7 81.7 %copy-start.1 = (bf16[8,128,512]{2,1,0:T(8,128)(2,1)S(1)}, bf16[8,128,512]{2,1,0:T(8,128)(2,1)}, u32[]{:S(2)}) copy-start(bf16[8,128,512]{2,1,0:T(8,128)(2,1)} %param.18) | copy-start | bytes 3145732
  (1 other events, 1.1 us)
where the time goes:
time: 410 us; the launch traced here: 408 us
  waiting for transfers between devices  187 us (46%)
  blocking collectives  72.3 us (18%)
  starting transfers between devices  58.9 us (14%)
  local copies, waits for them, and re-layouts  51.7 us (13%)
  matrix products  24.5 us (6%)
  other arithmetic  12.7 us (3%)
    all_to_all x1, waiting for transfers between devices, per_device(): lax.all_to_all(outgoing, 'wide', split_axis=0, concat_axis=0, tiled=True)  167 us
    unnamed x1, blocking collectives  72.3 us
    all_to_all x1, starting transfers between devices, per_device(): lax.all_to_all(latent_out, 'wide', split_axis=2, concat_axis=0, tiled=True)  40.7 us
    all_to_all x1, local copies, waits for them, and re-layouts, per_device(): lax.all_to_all(outgoing, 'wide', split_axis=0, concat_axis=0, tiled=True)  14.1 us
    all_to_all x1, waiting for transfers between devices, per_device(): lax.all_to_all(latent_out, 'wide', split_axis=2, concat_axis=0, tiled=True)  13.9 us
    squeeze x8, local copies, waits for them, and re-layouts, per_device(): state, _ = lax.scan(scan_step, start_state, (key_blocks, valid_blocks))  11.5 us
    gather x1, local copies, waits for them, and re-layouts, per_device(): prefill_blocks[source_row]  9.75 us
    while x40, local copies, waits for them, and re-layouts  8.8 us
  transfers between devices with their start and end apart: 4, of which 3 were waited for; matrix products, arithmetic and copies ran while one was open for 5% of the time, Pallas kernels for 0%

commit v1 on v0

--- a/solution.py
+++ b/solution.py
@@ -1,12 +1,475 @@
+import functools
 import math
 
 import jax
 import jax.numpy as jnp
 from jax import lax
+from jax.experimental import pallas as pl
+from jax.experimental.pallas import tpu as pltpu
 from jax.sharding import PartitionSpec as P
 
-
-def per_device(
+MIB = 1024 * 1024
+Z, Y, C = 4, 2, 2
+LOW = -1e30
+
+
+def place():
+    me = lax.axis_index("wide")
+    return me, me // (Y * C), (me // C) % Y, me % C
+
+
+def at(z, y, c):
+    return {"wide": (z * Y + y) * C + c}
+
+
+def remote(src, dst, send, recv, device):
+    return pltpu.make_async_remote_copy(
+        src_ref=src,
+        dst_ref=dst,
+        send_sem=send,
+        recv_sem=recv,
+        device_id=device,
+        device_id_type=pl.DeviceIdType.MESH,
+    )
+
+
+def greet(c, chip):
+    barrier = pltpu.get_barrier_semaphore()
+    others = [(lax.rem(chip + d, Z * Y)) * C + c for d in range(1, Z * Y)]
+    others.append(chip * C + 1 - c)
+    for other in others:
+        pl.semaphore_signal(
+            barrier, inc=1, device_id={"wide": other}, device_id_type=pl.DeviceIdType.MESH
+        )
+    pl.semaphore_wait(barrier, len(others))
+
+
+def gather_kernel(
+    q_own, blocks, meta, q_all, sib, metas,
+    local_sem, send_up, send_dn, send_y, recv_up, recv_dn, recv_y,
+    one_send, one_recv, meta_send, meta_recv,
+):
+    me, z, y, c = place()
+    chip = me // C
+    greet(c, chip)
+    sibling = at(z, y, 1 - c)
+
+    def row(zs, ys, cc):
+        return (zs * Y + ys) * C + (c if cc == 0 else 1 - c)
+
+    own_local = pltpu.make_async_copy(q_own.at[c], q_all.at[me], local_sem.at[0])
+    own_local.start()
+    to_sib = remote(q_own.at[1 - c], q_all.at[me], one_send.at[0], one_recv.at[0], sibling)
+    to_sib.start()
+    meta_local = pltpu.make_async_copy(meta, metas.at[chip], local_sem.at[1])
+    meta_local.start()
+    meta_copies = []
+    for d in range(1, Z * Y):
+        copy = remote(
+            meta, metas.at[chip], meta_send.at[d], meta_recv.at[d],
+            {"wide": lax.rem(chip + d, Z * Y) * C + c},
+        )
+        copy.start()
+        meta_copies.append(copy)
+    copy = remote(meta, metas.at[Z * Y], meta_send.at[0], meta_recv.at[0], sibling)
+    copy.start()
+    meta_copies.append(copy)
+
+    def up(d, cc):
+        r = row(z - d, y, cc)
+        src = q_own.at[c] if d == 0 and cc == 0 else q_all.at[r]
+        return remote(src, q_all.at[r], send_up.at[d, cc], recv_up.at[d, cc], at(z + 1, y, c))
+
+    def dn(d, cc):
+        r = row(z + d, y, cc)
+        src = q_own.at[c] if d == 0 and cc == 0 else q_all.at[r]
+        return remote(src, q_all.at[r], send_dn.at[d, cc], recv_dn.at[d, cc], at(z - 1, y, c))
+
+    def across(zs, cc, own=False):
+        r = row(zs, y, cc)
+        src = q_own.at[c] if own and cc == 0 else q_all.at[r]
+        return remote(src, q_all.at[r], send_y.at[zs, cc], recv_y.at[zs, cc], at(z, 1 - y, c))
+
+    key_copy = remote(blocks, sib, one_send.at[1], one_recv.at[1], sibling)
+    for cc in range(2):
+        if cc == 1:
+            to_sib.wait_recv()
+        pl.when(z < Z - 1)(lambda: up(0, cc).start())
+        pl.when(z > 0)(lambda: dn(0, cc).start())
+        across(z, cc, True).start()
+    key_copy.start()
+    for d in range(1, Z):
+        for cc in range(2):
+
+            @pl.when(z - d >= 0)
+            def _():
+                r = row(z - d, y, cc)
+                remote(
+                    q_all.at[r], q_all.at[r], send_up.at[d - 1, cc], recv_up.at[d - 1, cc], sibling
+                ).wait_recv()
+                if d < Z - 1:
+                    pl.when(z < Z - 1)(lambda: up(d, cc).start())
+                across(z - d, cc).start()
+
+            @pl.when(z + d < Z)
+            def _():
+                r = row(z + d, y, cc)
+                remote(
+                    q_all.at[r], q_all.at[r], send_dn.at[d - 1, cc], recv_dn.at[d - 1, cc], sibling
+                ).wait_recv()
+                if d < Z - 1:
+                    pl.when(z > 0)(lambda: dn(d, cc).start())
+                across(z + d, cc).start()
+
+    for zs in range(Z):
+        for cc in range(2):
+            r = row(zs, 1 - y, cc)
+            remote(
+                q_all.at[r], q_all.at[r], send_y.at[zs, cc], recv_y.at[zs, cc], sibling
+            ).wait_recv()
+            across(zs, cc).wait_send()
+    for d in range(Z - 1):
+        for cc in range(2):
+            pl.when((z - d >= 0) & (z < Z - 1))(lambda: up(d, cc).wait_send())
+            pl.when((z + d < Z) & (z > 0))(lambda: dn(d, cc).wait_send())
+    to_sib.wait_send()
+    key_copy.wait()
+    own_local.wait()
+    meta_local.wait()
+    for copy in meta_copies:
+        copy.wait()
+
+
+def attention_kernel(scale, steps, heads, table, limits, where, q_ref, *refs):
+    mine, theirs = refs[:8], refs[8:16]
+    fresh_ref, o_ref, m_ref, keys = refs[16:]
+    step = pl.program_id(0)
+    tok = mine[0].shape[1]
+    groups = q_ref.shape[0]
+    per = steps * heads
+    rows = groups * per
+    latent = o_ref.shape[2]
+    q_pair = q_ref[...].astype(jnp.float32)
+    keys[8 * tok :, :] = fresh_ref[...]
+    outs, maxes = [], []
+    lane = lax.broadcasted_iota(jnp.int32, (1, tok), 1)
+    lane_all = lax.broadcasted_iota(jnp.int32, (rows, tok), 1)
+    step_of = (lax.broadcasted_iota(jnp.int32, (rows, tok), 0) % per) // heads
+    for u in range(2):
+        k = step * 2 + u
+        query = q_pair[:, u * per : (u + 1) * per].reshape(rows, -1).astype(jnp.bfloat16)
+        for s in range(4):
+            keys[s * tok : (s + 1) * tok, :] = mine[u * 4 + s][0]
+            keys[(4 + s) * tok : (5 + s) * tok, :] = theirs[u * 4 + s][0]
+        scores = (
+            lax.dot_general(
+                query, keys[...], (((1,), (1,)), ((), ())), preferred_element_type=jnp.float32
+            )
+            * scale
+        )
+        parts = []
+        for s in range(8):
+            live = lane < limits[s // 4, k, s % 4]
+            parts.append(jnp.where(live, scores[:, s * tok : (s + 1) * tok], LOW))
+        bound = jnp.where(k == where[0], step_of, -1)
+        parts.append(jnp.where(lane_all <= bound, scores[:, 8 * tok :], LOW))
+        masked = jnp.concatenate(parts, axis=1)
+        top = jnp.maximum(jnp.max(masked, axis=1, keepdims=True), -1e29)
+        weights = jnp.exp(masked - top)
+        total = jnp.sum(weights, axis=1, keepdims=True)
+        out = jnp.dot(
+            weights.astype(jnp.bfloat16), keys[:, :latent], preferred_element_type=jnp.float32
+        )
+        outs.append(out.reshape(groups, per, latent))
+        stat = jnp.where(lane_all == 0, top, total)
+        maxes.append(stat.reshape(groups, per, tok))
+    o_ref[...] = jnp.concatenate(outs, axis=1).astype(jnp.bfloat16)
+    m_ref[...] = jnp.concatenate(maxes, axis=1)
+
+
+def reduce_kernel(
+    o_ref, stat_ref, out_ref,
+    stats, square, scaled, y_in, acc, up_in, dn_in, up_out, dn_out, fin, sib_in,
+    stat_send, stat_recv, send_y, recv_y, send_up, recv_up, send_dn, recv_dn, sib_send, sib_recv,
+):
+    me, z, y, c = place()
+    chip = me // C
+    greet(c, chip)
+    chips = Z * Y
+    stat_copies = []
+    for d in range(1, chips):
+        copy = remote(
+            stat_ref, stats.at[d], stat_send.at[d], stat_recv.at[d],
+            {"wide": lax.rem(chip + d, chips) * C + c},
+        )
+        copy.start()
+        stat_copies.append(copy)
+    groups = stat_ref.shape[1]
+    width = o_ref.shape[1]
+    square[...] = jnp.zeros_like(square)
+    stats[0] = stat_ref[...]
+    for copy in stat_copies:
+        copy.wait_recv()
+    top = stats[0, 0]
+    for d in range(1, chips):
+        top = jnp.maximum(top, stats[d, 0])
+    total = jnp.zeros_like(top)
+    for d in range(chips):
+        total += stats[d, 1] * jnp.exp(stats[d, 0] - top)
+    square[:groups, :width] = jnp.exp(stats[0, 0] - top) / total
+    square_t = square[...].T
+
+    f_all = square_t[:width, :groups]
+
+    def scale_chunk(base):
+        for cc in range(C):
+            j = base + cc
+            lanes = lax.broadcasted_iota(jnp.int32, f_all.shape, 1)
+            factor = jnp.sum(jnp.where(lanes == j, f_all, 0.0), axis=1, keepdims=True)
+            scaled[j] = (o_ref[j].astype(jnp.float32) * factor).astype(jnp.bfloat16)
+
+    order = (3, 0, 2, 1)
+
+    def y_copy(t):
+        base = (t * Y + 1 - y) * C
+        return remote(
+            scaled.at[pl.ds(base, C)], y_in.at[t], send_y.at[t], recv_y.at[t], at(z, 1 - y, c)
+        )
+
+    for t in order:
+        scale_chunk((t * Y + 1 - y) * C)
+        y_copy(t).start()
+    for t in order:
+        scale_chunk((t * Y + y) * C)
+
+    def up_copy(t):
+        return remote(
+            up_out.at[t], up_in.at[t], send_up.at[t], recv_up.at[t], at(z + 1, y, c)
+        )
+
+    def dn_copy(t):
+        return remote(
+            dn_out.at[t], dn_in.at[t], send_dn.at[t], recv_dn.at[t], at(z - 1, y, c)
+        )
+
+    def up_arrived(t):
+        remote(
+            up_out.at[t], up_in.at[t], send_up.at[t], recv_up.at[t], at(z, y, 1 - c)
+        ).wait_recv()
+
+    def dn_arrived(t):
+        remote(
+            dn_out.at[t], dn_in.at[t], send_dn.at[t], recv_dn.at[t], at(z, y, 1 - c)
+        ).wait_recv()
+
+    def get_y(t):
+        y_copy(t).wait_recv()
+        mine = scaled[pl.ds((t * Y + y) * C, C)].astype(jnp.float32)
+        acc[t] = mine + y_in[t].astype(jnp.float32)
+
+    def send_upward(t):
+        @pl.when(z == 0)
+        def _():
+            up_out[t] = acc[t].astype(jnp.bfloat16)
+
+        @pl.when((z > 0) & (z < t))
+        def _():
+            up_arrived(t)
+            up_out[t] = (acc[t] + up_in[t].astype(jnp.float32)).astype(jnp.bfloat16)
+
+        pl.when(z < t)(lambda: up_copy(t).start())
+
+    def send_downward(t):
+        @pl.when(z == Z - 1)
+        def _():
+            dn_out[t] = acc[t].astype(jnp.bfloat16)
+
+        @pl.when((z < Z - 1) & (z > t))
+        def _():
+            dn_arrived(t)
+            dn_out[t] = (acc[t] + dn_in[t].astype(jnp.float32)).astype(jnp.bfloat16)
+
+        pl.when(z > t)(lambda: dn_copy(t).start())
+
+    get_y(3)
+    send_upward(3)
+    get_y(0)
+    send_downward(0)
+    get_y(2)
+    send_upward(2)
+    get_y(1)
+    send_downward(1)
+    send_upward(1)
+    send_downward(2)
+    for t in range(Z):
+
+        @pl.when(z == t)
+        def _():
+            value = acc[t]
+            if t > 0:
+                up_arrived(t)
+                value = value + up_in[t].astype(jnp.float32)
+            if t < Z - 1:
+                dn_arrived(t)
+                value = value + dn_in[t].astype(jnp.float32)
+            fin[...] = value.astype(jnp.bfloat16)
+
+    swap = remote(fin.at[1 - c], sib_in, sib_send, sib_recv, at(z, y, 1 - c))
+    swap.start()
+    out_ref[c] = fin[c]
+    swap.wait()
+    out_ref[1 - c] = sib_in[...]
+    for t in range(Z):
+        y_copy(t).wait_send()
+        pl.when(z < t)(lambda: up_copy(t).wait_send())
+        pl.when(z > t)(lambda: dn_copy(t).wait_send())
+    for copy in stat_copies:
+        copy.wait_send()
+
+
+def move_queries(
+    prefill_blocks, block_owner, block_position, cache_len,
+    query_nope, query_rope, w_uk, w_uv, w_o, new_latent,
+):
+    members = lax.axis_size("wide")
+    slots, tok, width = prefill_blocks.shape
+    latent = w_uk.shape[2]
+    requests, steps, heads = query_nope.shape[:3]
+    per = steps * heads
+    half = members // C
+    rows = half * per
+    per_peer = (slots + members - 1) // members
+    me, z, y, c = place()
+    chip = me // C
+    scale = (query_nope.shape[3] + query_rope.shape[3]) ** (-0.5)
+
+    order = jnp.arange(slots)
+    same = (block_owner[:, None] == block_owner[None, :]) & (order[None, :] < order[:, None])
+    rank = jnp.sum(same.astype(jnp.int32), axis=1)
+    slot_of = jnp.where(block_owner >= 0, block_owner * per_peer + rank, members * per_peer)
+    matches = slot_of[None, :] == jnp.arange(members * per_peer)[:, None]
+    source = jnp.sum(jnp.where(matches, order[None, :], 0), axis=1)
+    place_of = jnp.sum(jnp.where(matches, block_position[None, :] + 1, 0), axis=1)
+    channels = members * per_peer
+    meta = jnp.concatenate(
+        [
+            jnp.concatenate([source, place_of])[None, :],
+            jnp.broadcast_to(cache_len[:1, None], (7, 2 * channels)),
+        ]
+    ).astype(jnp.int32)
+
+    q_latent = jnp.einsum(
+        "rshn,hnc->rshc", query_nope, w_uk, preferred_element_type=jnp.float32
+    ).astype(jnp.bfloat16)
+    q_full = jnp.concatenate([q_latent, query_rope], axis=3)
+    q_own = q_full.reshape(half, C, per, width).transpose(1, 0, 2, 3).reshape(C, rows, width)
+
+    anywhere = pl.BlockSpec(memory_space=pl.ANY)
+    vmem = pl.BlockSpec(memory_space=pltpu.VMEM)
+    dma = pltpu.SemaphoreType.DMA
+    q_all, sib, metas = pl.pallas_call(
+        gather_kernel,
+        out_shape=(
+            jax.ShapeDtypeStruct((members, rows, width), jnp.bfloat16),
+            jax.ShapeDtypeStruct(prefill_blocks.shape, jnp.bfloat16),
+            jax.ShapeDtypeStruct((half + 1,) + meta.shape, jnp.int32),
+        ),
+        in_specs=[anywhere] * 3,
+        out_specs=(anywhere,) * 3,
+        scratch_shapes=[
+            dma((2,)),
+            dma((Z, 2)), dma((Z, 2)), dma((Z, 2)),
+            dma((Z, 2)), dma((Z, 2)), dma((Z, 2)),
+            dma((2,)), dma((2,)), dma((half,)), dma((half,)),
+        ],
+        compiler_params=pltpu.CompilerParams(collective_id=0, has_side_effects=True),
+        name="gather_queries",
+    )(q_own, prefill_blocks, meta)
+
+    def my_side(tag_row):
+        both = tag_row[0].reshape(2, half, C, per_peer)
+        return jnp.where(c == 0, both[:, :, 0], both[:, :, 1])
+
+    mine, theirs = my_side(meta), my_side(metas[half])
+    table = jnp.stack([mine[0], theirs[0]])
+    spots = jnp.stack([mine[1], theirs[1]])
+    lengths = metas[:half, 1, 0]
+    limits = jnp.where(spots > 0, lengths[None, :, None] - (spots - 1) * tok, 0)
+    fresh = jnp.zeros((tok, width), jnp.bfloat16).at[:steps].set(new_latent[0])
+
+    def key_spec(side, u, s):
+        return pl.BlockSpec(
+            (1, tok, width), lambda g, table, limits, where: (table[side, 2 * g + u, s], 0, 0)
+        )
+
+    pairs = [(u, s) for u in range(2) for s in range(per_peer)]
+    partial, stat = pl.pallas_call(
+        functools.partial(attention_kernel, scale, steps, heads),
+        out_shape=(
+            jax.ShapeDtypeStruct((members, rows, latent), jnp.bfloat16),
+            jax.ShapeDtypeStruct((members, rows, tok), jnp.float32),
+        ),
+        grid_spec=pltpu.PrefetchScalarGridSpec(
+            num_scalar_prefetch=3,
+            grid=(half // 2,),
+            in_specs=[pl.BlockSpec((members, 2 * per, width), lambda g, *_: (0, g, 0))]
+            + [key_spec(0, u, s) for u, s in pairs]
+            + [key_spec(1, u, s) for u, s in pairs]
+            + [pl.BlockSpec((tok, width), lambda g, *_: (0, 0))],
+            out_specs=(
+                pl.BlockSpec((members, 2 * per, latent), lambda g, *_: (0, g, 0)),
+                pl.BlockSpec((members, 2 * per, tok), lambda g, *_: (0, g, 0)),
+            ),
+            scratch_shapes=[pltpu.VMEM(((2 * per_peer + 1) * tok, width), jnp.bfloat16)],
+        ),
+        compiler_params=pltpu.CompilerParams(vmem_limit_bytes=48 * MIB),
+        name="partial_attention",
+    )(
+        table, limits, chip.reshape(1), q_all,
+        *([prefill_blocks] * len(pairs)), *([sib] * len(pairs)), fresh,
+    )
+    stat_rows = stat[:, :, :2].transpose(2, 0, 1)
+
+    chunk = (C, rows, latent)
+    gathered = pl.pallas_call(
+        reduce_kernel,
+        out_shape=jax.ShapeDtypeStruct((C, rows, latent), jnp.bfloat16),
+        in_specs=[vmem, vmem],
+        out_specs=vmem,
+        scratch_shapes=[
+            pltpu.VMEM((half, 2, members, rows), jnp.float32),
+            pltpu.VMEM((128, 256), jnp.float32),
+            pltpu.VMEM((members, rows, latent), jnp.bfloat16),
+            pltpu.VMEM((Z,) + chunk, jnp.bfloat16),
+            pltpu.VMEM((Z,) + chunk, jnp.float32),
+            pltpu.VMEM((Z,) + chunk, jnp.bfloat16),
+            pltpu.VMEM((Z,) + chunk, jnp.bfloat16),
+            pltpu.VMEM((Z,) + chunk, jnp.bfloat16),
+            pltpu.VMEM((Z,) + chunk, jnp.bfloat16),
+            pltpu.VMEM(chunk, jnp.bfloat16),
+            pltpu.VMEM(chunk[1:], jnp.bfloat16),
+            dma((half,)), dma((half,)),
+            dma((Z,)), dma((Z,)), dma((Z,)), dma((Z,)), dma((Z,)), dma((Z,)),
+            dma, dma,
+        ],
+        compiler_params=pltpu.CompilerParams(
+            collective_id=1, has_side_effects=True, vmem_limit_bytes=48 * MIB
+        ),
+        name="reduce_partials",
+    )(partial, stat_rows)
+
+    latents = gathered.reshape(C, half, steps, heads, latent)
+    values = jnp.einsum(
+        "pkshc,hcv->kpshv", latents, w_uv, preferred_element_type=jnp.float32
+    ).astype(jnp.bfloat16)
+    values = values.reshape(members * steps, -1)
+    share = jnp.dot(values, w_o, preferred_element_type=jnp.float32).astype(jnp.bfloat16)
+    share = share.reshape(members, steps, -1)
+    shares = lax.all_to_all(share, "wide", split_axis=0, concat_axis=0, tiled=True)
+    return jnp.sum(shares.astype(jnp.float32), axis=0, keepdims=True).astype(jnp.bfloat16)
+
+
+def move_keys(
     prefill_blocks,
     block_owner,
     block_position,
@@ -127,6 +590,7 @@
         P("wide", None),
         P(("groups", "wide"), None, None),
     )
+    per_device = move_queries if mesh.shape["wide"] == Z * Y * C else move_keys
     out_specs = P(("groups", "wide"), None, None)
     return jax.shard_map(
         per_device, mesh=mesh, in_specs=in_specs, out_specs=out_specs, check_vma=False

time: 410 us -> 199 us (0.49)
  waiting for transfers between devices: 187 us -> 0 us
  Pallas kernels: 0 us -> 121 us
  starting transfers between devices: 58.9 us -> 0 us
  blocking collectives: 72.3 us -> 36 us
  local copies, waits for them, and re-layouts: 51.7 us -> 25.3 us
  matrix products: 24.5 us -> 10.6 us
  other arithmetic: 12.7 us -> 3.66 us
    all_to_all x4 -> x0, waiting for transfers between devices: 187 us -> none  [the longest x1 167 us: per_device(): lax.all_to_all(outgoing, 'wide', split_axis=0, concat_axis=0, tiled=True)]
    pallas_call x0 -> x3, Pallas kernels: none -> 121 us  [the longest x1 51.2 us: move_queries(): pl.pallas_call(reduce_kernel, out_shape=jax.ShapeDtypeStruct((C, rows, la...]
    unnamed x1 -> x0, blocking collectives: 72.3 us -> none
    all_to_all x4 -> x0, starting transfers between devices: 58.9 us -> none  [the longest x1 40.7 us: per_device(): lax.all_to_all(latent_out, 'wide', split_axis=2, concat_axis=0, tiled=True)]
    all_to_all x0 -> x1, blocking collectives: none -> 36 us  [move_queries(): lax.all_to_all(share, 'wide', split_axis=0, concat_axis=0, tiled=True)]
    unnamed x12 -> x11, local copies, waits for them, and re-layouts: 1.52 us -> 18.5 us
    all_to_all x2 -> x0, local copies, waits for them, and re-layouts: 14.1 us -> none  [the longest x1 14.1 us: per_device(): lax.all_to_all(outgoing, 'wide', split_axis=0, concat_axis=0, tiled=True)]
    dot_general x21 -> x3, matrix products: 24.5 us -> 10.6 us  [the longest x1 7.83 us: move_queries(): jnp.dot(values, w_o, preferred_element_type=jnp.float32)]
  transfers between devices with their start and end apart: 4 -> 0, of which waited for: 3 -> 0; matrix products, arithmetic and copies ran while one was open for 5% -> 0% of each run, Pallas kernels for 0% -> 0%
where the time goes in v1:
time: 199 us; the launch traced here: 198 us
  Pallas kernels  121 us (61%)
  blocking collectives  36 us (18%)
  local copies, waits for them, and re-layouts  25.3 us (13%)
  matrix products  10.6 us (5%)
  other arithmetic  3.66 us (2%)
    pallas_call x1, Pallas kernels, move_queries(): pl.pallas_call(reduce_kernel, out_shape=jax.ShapeDtypeStruct((C, rows, la...  51.2 us
    pallas_call x1, Pallas kernels, move_queries(): pl.pallas_call(gather_kernel, out_shape=(jax.ShapeDtypeStruct((members, r...  50.6 us
    all_to_all x1, blocking collectives, move_queries(): lax.all_to_all(share, 'wide', split_axis=0, concat_axis=0, tiled=True)  36 us
    pallas_call x1, Pallas kernels, move_queries(): pl.pallas_call(functools.partial(attention_kernel, scale, steps, heads),...  19.5 us
    unnamed x11, local copies, waits for them, and re-layouts  18.5 us
    dot_general x1, matrix products, move_queries(): jnp.dot(values, w_o, preferred_element_type=jnp.float32)  7.83 us

profile of v1, /device:TPU:0, one launch (start us, length us, event | category | flops | bytes accessed | tf_op | source)
XLA Modules:
  0.0 197.7 jit_solution(8126071768230329892)
XLA Ops:
  0.0 0.7 broadcast_add_fusion
  0.7 0.9 convert_reduce_fusion
  1.7 0.7 compare_select_fusion
  2.3 0.1 select_reduce_fusion.1
  3.4 0.9 copy.58
  4.3 1.2 fusion
  5.6 0.9 copy.60
  6.5 14.1 %copy.61.blocks.refs_0_.refs_1_.refs_2_.refs_3_.refs_4_.refs_5_.refs_6_.refs_7_ = bf16[64,128,576]{2,1,0:T(8,128)(2,1)} copy(bf16[64,128,576]{1,2,0:T(8,128)(2,1)} %param.12) | data formatting | bytes 18874368 | tf_op args[0]
  20.6 0.6 concatenate.23.meta
  21.2 50.6 %gather_queries.1 = (bf16[16,192,576]{2,1,0:T(8,128)(2,1)}, bf16[64,128,576]{2,1,0:T(8,128)(2,1)}, s32[9,8,128]{2,1,0:T(8,128)}) custom-call(bf16[2,192,576]{2,1,0:T(8,128)(2,1)} %bitcast.39, bf16[64,128,576]{2,1,0:T(8,128)(2,1)} %copy.61.blocks.refs_0_.refs_1_.refs_2_.refs_3_.refs_4_.refs_5_.refs_6_.refs_7_, s32[8,128]{1,0:T(8,128)} %concatenate.23.meta), custom_call_target="tpu_custom_call" | custom-call | tf_op jit(solution)/shard_map/gather_queries/pallas_call | solution.py:370
  71.8 1.0 slice_reduce_fusion
  72.8 0.7 slice_reduce_fusion.1
  73.5 0.1 reshape_squeeze.3
  73.8 19.5 %partial_attention.1 = (bf16[16,192,512]{2,1,0:T(8,128)(2,1)S(1)}, f32[16,192,128]{2,1,0:T(8,128)S(1)}) custom-call(s32[2,8,4]{2,1,0:T(8,128)S(1)} %pad_add_fusion.table, s32[2,8,4]{2,1,0:T(8,128)S(1)} %subtract_select_fusion.limits, s32[1]{0:T(128)} %bitcast.12.where, bf16[16,192,576]{2,1,0:T(8,128)(2,1)} %get-tuple-element.23.q_ref, ...), custom_call_target="tpu_custom_call" | custom-call | tf_op jit(solution)/shard_map/partial_attention/pallas_call | solution.py:406
  93.3 1.7 copy-done.1
  95.0 1.9 copy.77
  96.9 0.8 slice_bitcast_fusion.stat_ref
  97.7 1.9 copy-done.2
  99.6 51.2 %reduce_partials.1 = bf16[2,192,512]{2,1,0:T(8,128)(2,1)S(1)} custom-call(bf16[16,192,512]{2,1,0:T(8,128)(2,1)S(1)} %copy-done.2, f32[2,16,192]{2,1,0:T(8,128)S(1)} %slice_bitcast_fusion.stat_ref), custom_call_target="tpu_custom_call" | custom-call | tf_op jit(solution)/shard_map/reduce_partials/pallas_call | solution.py:434
  150.8 1.6 fusion.1
  152.4 7.8 %convolution_convert_fusion = bf16[48,7168]{1,0:T(8,128)(2,1)S(1)} fusion(bf16[1024,7168]{1,0:T(8,128)(2,1)} %param.20, bf16[6,8,8,128]{3,2,1,0:T(8,128)(2,1)S(1)} %bitcast.41), kind=kOutput, calls=%fused_computation | convolution fusion | flops 704987136 | bytes 15466496 | tf_op jit(solution)/shard_map/dot_general | solution.py:466
  160.2 0.4 reshape.80
  160.7 36.0 %all_to_all.5 = bf16[16,3,7168]{2,1,0:T(4,128)(2,1)S(1)} all-to-all(bf16[16,3,7168]{2,1,0:T(4,128)(2,1)S(1)} %reshape.80), channel_id=1, replica_groups=mesh['groups'=2,'wide'=16] {'wide'}, dimensions={0} | all-to-all | bytes 1376256 | tf_op jit(solution)/shard_map/all_to_all | solution.py:468
  196.7 1.0 reduce_sum.42
  (20 shorter events, 0.6 us)
Async XLA Ops:
  0.0 4.3 %copy-start = (bf16[8,128,512]{2,1,0:T(8,128)(2,1)S(1)}, bf16[8,128,512]{2,1,0:T(8,128)(2,1)}, u32[]{:S(2)}) copy-start(bf16[8,128,512]{2,1,0:T(8,128)(2,1)} %param.18) | copy-start | bytes 3145732
  20.6 53.1 %copy-start.3 = (bf16[1,3,576]{2,1,0:T(4,128)(2,1)S(1)}, bf16[1,3,576]{2,1,0:T(4,128)(2,1)}, u32[]{:S(2)}) copy-start(bf16[1,3,576]{2,1,0:T(4,128)(2,1)} %param.21) | copy-start | bytes 10372
  93.3 1.7 copy-start.1
  97.7 1.9 copy-start.2

commit v2 on v1

--- a/solution.py
+++ b/solution.py
@@ -144,13 +144,13 @@
     mine, theirs = refs[:8], refs[8:16]
     fresh_ref, o_ref, m_ref, keys = refs[16:]
     step = pl.program_id(0)
-    tok = mine[0].shape[1]
+    tok = mine[0].shape[2]
     groups = q_ref.shape[0]
     per = steps * heads
     rows = groups * per
     latent = o_ref.shape[2]
     q_pair = q_ref[...].astype(jnp.float32)
-    keys[8 * tok :, :] = fresh_ref[...]
+    keys[:, 8 * tok :] = fresh_ref[...]
     outs, maxes = [], []
     lane = lax.broadcasted_iota(jnp.int32, (1, tok), 1)
     lane_all = lax.broadcasted_iota(jnp.int32, (rows, tok), 1)
@@ -159,12 +159,10 @@
         k = step * 2 + u
         query = q_pair[:, u * per : (u + 1) * per].reshape(rows, -1).astype(jnp.bfloat16)
         for s in range(4):
-            keys[s * tok : (s + 1) * tok, :] = mine[u * 4 + s][0]
-            keys[(4 + s) * tok : (5 + s) * tok, :] = theirs[u * 4 + s][0]
+            keys[:, s * tok : (s + 1) * tok] = mine[u * 4 + s][0]
+            keys[:, (4 + s) * tok : (5 + s) * tok] = theirs[u * 4 + s][0]
         scores = (
-            lax.dot_general(
-                query, keys[...], (((1,), (1,)), ((), ())), preferred_element_type=jnp.float32
-            )
+            jnp.dot(query, keys[...], preferred_element_type=jnp.float32)
             * scale
         )
         parts = []
@@ -177,8 +175,11 @@
         top = jnp.maximum(jnp.max(masked, axis=1, keepdims=True), -1e29)
         weights = jnp.exp(masked - top)
         total = jnp.sum(weights, axis=1, keepdims=True)
-        out = jnp.dot(
-            weights.astype(jnp.bfloat16), keys[:, :latent], preferred_element_type=jnp.float32
+        out = lax.dot_general(
+            weights.astype(jnp.bfloat16),
+            keys[:latent, :],
+            (((1,), (1,)), ((), ())),
+            preferred_element_type=jnp.float32,
         )
         outs.append(out.reshape(groups, per, latent))
         stat = jnp.where(lane_all == 0, top, total)
@@ -188,9 +189,11 @@
 
 
 def reduce_kernel(
-    o_ref, stat_ref, out_ref,
+    steps, heads, o_ref, stat_ref, w_uv_ref, w_o_ref, out_ref,
     stats, square, scaled, y_in, acc, up_in, dn_in, up_out, dn_out, fin, sib_in,
+    w_o, part, part_in, rows_f, message, inbox,
     stat_send, stat_recv, send_y, recv_y, send_up, recv_up, send_dn, recv_dn, sib_send, sib_recv,
+    load_sem, part_send, part_recv, row_send, row_recv,
 ):
     me, z, y, c = place()
     chip = me // C
@@ -204,6 +207,8 @@
         )
         copy.start()
         stat_copies.append(copy)
+    load = pltpu.make_async_copy(w_o_ref, w_o, load_sem)
+    load.start()
     groups = stat_ref.shape[1]
     width = o_ref.shape[1]
     square[...] = jnp.zeros_like(square)
@@ -316,9 +321,58 @@
 
     swap = remote(fin.at[1 - c], sib_in, sib_send, sib_recv, at(z, y, 1 - c))
     swap.start()
-    out_ref[c] = fin[c]
+    per = chips * steps
     swap.wait()
-    out_ref[1 - c] = sib_in[...]
+    even = jnp.where(c == 0, fin[c], sib_in[...])
+    odd = jnp.where(c == 0, sib_in[...], fin[c])
+    both = jnp.concatenate([even, odd], axis=0)
+    row_head = lax.broadcasted_iota(jnp.int32, (both.shape[0], w_uv_ref.shape[2]), 0) % heads
+    values = []
+    for h in range(heads):
+        every = jnp.dot(both, w_uv_ref[h], preferred_element_type=jnp.float32)
+        every = jnp.where(row_head == h, every, 0.0)
+        values.append(jnp.sum(every.reshape(C * per, heads, -1), axis=1))
+    values = jnp.concatenate(values, axis=1).astype(jnp.bfloat16)
+    rows_f[...] = jnp.zeros_like(rows_f)
+    load.wait()
+    tiles, _, wide = part_in.shape
+
+    def part_copy(i):
+        return remote(
+            part.at[1 - c, i], part_in.at[i], part_send.at[i], part_recv.at[i], at(z, y, 1 - c)
+        )
+
+    for i in range(tiles):
+        share = jnp.dot(
+            values, w_o[:, i * wide : (i + 1) * wide], preferred_element_type=jnp.float32
+        )
+        part[0, i] = share[:per]
+        part[1, i] = share[per:]
+        part_copy(i).start()
+    for i in range(tiles):
+        part_copy(i).wait_recv()
+        summed = part[c, i] + part_in[i]
+        for k in range(chips):
+            rows_f[k, i * steps : (i + 1) * steps, :] = summed[k * steps : (k + 1) * steps]
+    message[...] = rows_f[...].astype(jnp.bfloat16)
+    row_copies = []
+    for d in range(1, chips):
+        other = lax.rem(chip + d, chips)
+        copy = remote(
+            message.at[other], inbox.at[d - 1], row_send.at[d - 1], row_recv.at[d - 1],
+            {"wide": other * C + c},
+        )
+        copy.start()
+        row_copies.append(copy)
+    result = rows_f[chip]
+    for d in range(1, chips):
+        row_copies[d - 1].wait_recv()
+        result = result + inbox[d - 1].astype(jnp.float32)
+    out_ref[...] = result.astype(jnp.bfloat16)
+    for i in range(tiles):
+        part_copy(i).wait_send()
+    for copy in row_copies:
+        copy.wait_send()
     for t in range(Z):
         y_copy(t).wait_send()
         pl.when(z < t)(lambda: up_copy(t).wait_send())
@@ -339,6 +393,7 @@
     half = members // C
     rows = half * per
     per_peer = (slots + members - 1) // members
+    blocks_t = jnp.swapaxes(prefill_blocks, 1, 2)
     me, z, y, c = place()
     chip = me // C
     scale = (query_nope.shape[3] + query_rope.shape[3]) ** (-0.5)
@@ -371,7 +426,7 @@
         gather_kernel,
         out_shape=(
             jax.ShapeDtypeStruct((members, rows, width), jnp.bfloat16),
-            jax.ShapeDtypeStruct(prefill_blocks.shape, jnp.bfloat16),
+            jax.ShapeDtypeStruct(blocks_t.shape, jnp.bfloat16),
             jax.ShapeDtypeStruct((half + 1,) + meta.shape, jnp.int32),
         ),
         in_specs=[anywhere] * 3,
@@ -384,7 +439,7 @@
         ],
         compiler_params=pltpu.CompilerParams(collective_id=0, has_side_effects=True),
         name="gather_queries",
-    )(q_own, prefill_blocks, meta)
+    )(q_own, blocks_t, meta)
 
     def my_side(tag_row):
         both = tag_row[0].reshape(2, half, C, per_peer)
@@ -395,11 +450,11 @@
     spots = jnp.stack([mine[1], theirs[1]])
     lengths = metas[:half, 1, 0]
     limits = jnp.where(spots > 0, lengths[None, :, None] - (spots - 1) * tok, 0)
-    fresh = jnp.zeros((tok, width), jnp.bfloat16).at[:steps].set(new_latent[0])
+    fresh = jnp.zeros((width, tok), jnp.bfloat16).at[:, :steps].set(new_latent[0].T)
 
     def key_spec(side, u, s):
         return pl.BlockSpec(
-            (1, tok, width), lambda g, table, limits, where: (table[side, 2 * g + u, s], 0, 0)
+            (1, width, tok), lambda g, table, limits, where: (table[side, 2 * g + u, s], 0, 0)
         )
 
     pairs = [(u, s) for u in range(2) for s in range(per_peer)]
@@ -415,26 +470,30 @@
             in_specs=[pl.BlockSpec((members, 2 * per, width), lambda g, *_: (0, g, 0))]
             + [key_spec(0, u, s) for u, s in pairs]
             + [key_spec(1, u, s) for u, s in pairs]
-            + [pl.BlockSpec((tok, width), lambda g, *_: (0, 0))],
+            + [pl.BlockSpec((width, tok), lambda g, *_: (0, 0))],
             out_specs=(
                 pl.BlockSpec((members, 2 * per, latent), lambda g, *_: (0, g, 0)),
                 pl.BlockSpec((members, 2 * per, tok), lambda g, *_: (0, g, 0)),
             ),
-            scratch_shapes=[pltpu.VMEM(((2 * per_peer + 1) * tok, width), jnp.bfloat16)],
+            scratch_shapes=[pltpu.VMEM((width, (2 * per_peer + 1) * tok), jnp.bfloat16)],
         ),
         compiler_params=pltpu.CompilerParams(vmem_limit_bytes=48 * MIB),
         name="partial_attention",
     )(
         table, limits, chip.reshape(1), q_all,
-        *([prefill_blocks] * len(pairs)), *([sib] * len(pairs)), fresh,
+        *([blocks_t] * len(pairs)), *([sib] * len(pairs)), fresh,
     )
     stat_rows = stat[:, :, :2].transpose(2, 0, 1)
 
     chunk = (C, rows, latent)
-    gathered = pl.pallas_call(
-        reduce_kernel,
-        out_shape=jax.ShapeDtypeStruct((C, rows, latent), jnp.bfloat16),
-        in_specs=[vmem, vmem],
+    model = w_o.shape[1]
+    tile = math.gcd(model, 512)
+    tiles = model // tile
+    tall = (tiles * steps + 15) // 16 * 16
+    out = pl.pallas_call(
+        functools.partial(reduce_kernel, steps, heads),
+        out_shape=jax.ShapeDtypeStruct((tall, tile), jnp.bfloat16),
+        in_specs=[vmem, vmem, vmem, anywhere],
         out_specs=vmem,
         scratch_shapes=[
             pltpu.VMEM((half, 2, members, rows), jnp.float32),
@@ -448,25 +507,24 @@
             pltpu.VMEM((Z,) + chunk, jnp.bfloat16),
             pltpu.VMEM(chunk, jnp.bfloat16),
             pltpu.VMEM(chunk[1:], jnp.bfloat16),
+            pltpu.VMEM(w_o.shape, jnp.bfloat16),
+            pltpu.VMEM((C, tiles, half * steps, tile), jnp.float32),
+            pltpu.VMEM((tiles, half * steps, tile), jnp.float32),
+            pltpu.VMEM((half, tall, tile), jnp.float32),
+            pltpu.VMEM((half, tall, tile), jnp.bfloat16),
+            pltpu.VMEM((half - 1, tall, tile), jnp.bfloat16),
             dma((half,)), dma((half,)),
             dma((Z,)), dma((Z,)), dma((Z,)), dma((Z,)), dma((Z,)), dma((Z,)),
             dma, dma,
+            dma, dma((tiles,)), dma((tiles,)), dma((half,)), dma((half,)),
         ],
         compiler_params=pltpu.CompilerParams(
-            collective_id=1, has_side_effects=True, vmem_limit_bytes=48 * MIB
+            collective_id=1, has_side_effects=True, vmem_limit_bytes=56 * MIB
         ),
         name="reduce_partials",
-    )(partial, stat_rows)
-
-    latents = gathered.reshape(C, half, steps, heads, latent)
-    values = jnp.einsum(
-        "pkshc,hcv->kpshv", latents, w_uv, preferred_element_type=jnp.float32
-    ).astype(jnp.bfloat16)
-    values = values.reshape(members * steps, -1)
-    share = jnp.dot(values, w_o, preferred_element_type=jnp.float32).astype(jnp.bfloat16)
-    share = share.reshape(members, steps, -1)
-    shares = lax.all_to_all(share, "wide", split_axis=0, concat_axis=0, tiled=True)
-    return jnp.sum(shares.astype(jnp.float32), axis=0, keepdims=True).astype(jnp.bfloat16)
+    )(partial, stat_rows, w_uv, w_o)
+    out = out[: tiles * steps].reshape(tiles, steps, tile).transpose(1, 0, 2)
+    return out.reshape(1, steps, model)
 
 
 def move_keys(

time: 199 us -> 168 us (0.84)
  blocking collectives: 36 us -> 0 us
  Pallas kernels: 121 us -> 149 us
  local copies, waits for them, and re-layouts: 25.3 us -> 11.8 us
  matrix products: 10.6 us -> 1.17 us
    all_to_all x1 -> x0, blocking collectives: 36 us -> none  [move_queries(): lax.all_to_all(share, 'wide', split_axis=0, concat_axis=0, tiled=True)]
    pallas_call x1, Pallas kernels: 51.2 us -> 78.5 us  [move_queries(): pl.pallas_call(functools.partial(reduce_kernel, steps, heads), out_shape=...]
    unnamed x11 -> x7, local copies, waits for them, and re-layouts: 18.5 us -> 3.45 us
    dot_general x2 -> x0, matrix products: 9.39 us -> none  [the longest x1 7.83 us: move_queries(): jnp.dot(values, w_o, preferred_element_type=jnp.float32)]
where the time goes in v2:
time: 168 us; the launch traced here: 167 us
  Pallas kernels  149 us (89%)
  local copies, waits for them, and re-layouts  11.8 us (7%)
  other arithmetic  3.99 us (2%)
    pallas_call x1, Pallas kernels, move_queries(): pl.pallas_call(functools.partial(reduce_kernel, steps, heads), out_shape=...  78.5 us
    pallas_call x1, Pallas kernels, move_queries(): pl.pallas_call(gather_kernel, out_shape=(jax.ShapeDtypeStruct((members, r...  50.6 us
    pallas_call x1, Pallas kernels, move_queries(): pl.pallas_call(functools.partial(attention_kernel, scale, steps, heads),...  20.1 us
    unnamed x7, local copies, waits for them, and re-layouts  3.45 us

profile of v2, /device:TPU:0, one launch (start us, length us, event | category | flops | bytes accessed | tf_op | source)
XLA Modules:
  0.0 166.9 jit_solution(10400710002905741227)
XLA Ops:
  0.0 0.7 compare_reduce_fusion
  1.4 0.7 broadcast_add_fusion
  2.0 0.9 convert_reduce_fusion
  2.9 0.7 compare_select_fusion
  3.6 0.1 select_reduce_fusion.1
  3.8 0.6 concatenate.23.meta
  4.4 0.1 concatenate.18
  4.5 0.1 concatenate.19
  4.6 0.9 copy.40
  5.5 0.9 copy.50
  6.4 0.7 select_bitcast_fusion
  7.2 1.2 fusion
  8.4 0.1 copy.41
  8.5 0.9 copy.42
  9.4 50.6 %gather_queries.1 = (bf16[16,192,576]{2,1,0:T(8,128)(2,1)}, bf16[64,576,128]{2,1,0:T(8,128)(2,1)}, s32[9,8,128]{2,1,0:T(8,128)}) custom-call(bf16[2,192,576]{2,1,0:T(8,128)(2,1)} %bitcast.40, bf16[64,576,128]{2,1,0:T(8,128)(2,1)} %bitcast.31, s32[8,128]{1,0:T(8,128)} %concatenate.23.meta), custom_call_target="tpu_custom_call" | custom-call | tf_op jit(solution)/shard_map/gather_queries/pallas_call | solution.py:425
  60.0 1.0 slice_reduce_fusion
  61.0 0.7 slice_reduce_fusion.1
  61.7 0.1 reshape_squeeze.3
  61.9 20.1 %partial_attention.1 = (bf16[16,192,512]{2,1,0:T(8,128)(2,1)S(1)}, f32[16,192,128]{2,1,0:T(8,128)S(1)}) custom-call(s32[2,8,4]{2,1,0:T(8,128)S(1)} %pad_add_fusion.table, s32[2,8,4]{2,1,0:T(8,128)S(1)} %subtract_select_fusion.limits, s32[1]{0:T(128)} %bitcast.13.where, bf16[16,192,576]{2,1,0:T(8,128)(2,1)} %get-tuple-element.23.q_ref, ...), custom_call_target="tpu_custom_call" | custom-call | tf_op jit(solution)/shard_map/partial_attention/pallas_call | solution.py:461
  82.0 1.7 copy-done.1
  83.7 1.9 %copy.51 = f32[16,192,128]{1,0,2:T(8,128)} copy(f32[16,192,128]{2,1,0:T(8,128)S(1)} %get-tuple-element.26) | data formatting | bytes 3145728 | tf_op jit(solution)/shard_map/partial_attention/pallas_call | solution.py:461
  85.6 1.4 slice_bitcast_fusion.stat_ref
  87.0 78.5 %reduce_partials.1 = bf16[48,512]{1,0:T(8,128)(2,1)} custom-call(bf16[16,192,512]{2,1,0:T(8,128)(2,1)} %copy-done.1, f32[2,16,192]{2,1,0:T(8,128)} %slice_bitcast_fusion.stat_ref, bf16[8,512,128]{2,1,0:T(8,128)(2,1)} %w_uv_ref.1, bf16[1024,7168]{1,0:T(8,128)(2,1)} %w_o_ref.1), custom_call_target="tpu_custom_call" | custom-call | tf_op jit(solution)/shard_map/reduce_partials/pallas_call | solution.py:493
  165.4 1.5 reshape.69
  (13 shorter events, 0.3 us)
Async XLA Ops:
  0.0 7.2 %copy-start = (bf16[8,128,512]{2,1,0:T(8,128)(2,1)S(1)}, bf16[8,128,512]{2,1,0:T(8,128)(2,1)}, u32[]{:S(2)}) copy-start(bf16[8,128,512]{2,1,0:T(8,128)(2,1)} %param.18) | copy-start | bytes 3145732
  82.0 1.7 copy-start.1

commit v3 on v2

--- a/solution.py
+++ b/solution.py
@@ -44,132 +44,166 @@
     pl.semaphore_wait(barrier, len(others))
 
 
-def gather_kernel(
-    q_own, blocks, meta, q_all, sib, metas,
+PHASES = 4
+
+
+def attend_kernel(
+    scale, steps, heads, q_own, blocks, meta, fresh_ref, o_ref, m_ref,
+    q_all, mine, theirs, metas, tags, keys,
     local_sem, send_up, send_dn, send_y, recv_up, recv_dn, recv_y,
-    one_send, one_recv, meta_send, meta_recv,
+    q_send, q_recv, key_send, key_recv, meta_send, meta_recv,
 ):
     me, z, y, c = place()
     chip = me // C
+    chips = Z * Y
+    sibling = at(z, y, 1 - c)
+    load = pltpu.make_async_copy(blocks, mine, local_sem.at[0])
+    load.start()
+    own_local = pltpu.make_async_copy(q_own.at[c], q_all.at[me], local_sem.at[1])
+    own_local.start()
+    meta_local = pltpu.make_async_copy(meta, metas.at[chip], local_sem.at[2])
+    meta_local.start()
     greet(c, chip)
-    sibling = at(z, y, 1 - c)
+    groups, rows, _ = q_all.shape
+    piece = rows // PHASES
+    per = steps * heads
+    tok = mine.shape[2]
+    latent = o_ref.shape[2]
 
     def row(zs, ys, cc):
         return (zs * Y + ys) * C + (c if cc == 0 else 1 - c)
 
-    own_local = pltpu.make_async_copy(q_own.at[c], q_all.at[me], local_sem.at[0])
-    own_local.start()
-    to_sib = remote(q_own.at[1 - c], q_all.at[me], one_send.at[0], one_recv.at[0], sibling)
-    to_sib.start()
-    meta_local = pltpu.make_async_copy(meta, metas.at[chip], local_sem.at[1])
-    meta_local.start()
+    def cut(ref, r, g):
+        return ref.at[r, pl.ds(g * piece, piece)]
+
+    def to_sib(g):
+        return remote(
+            cut(q_own, 1 - c, g), cut(q_all, me, g), q_send.at[g], q_recv.at[g], sibling
+        )
+
+    def source(d, cc, r, g):
+        return cut(q_own, c, g) if d == 0 and cc == 0 else cut(q_all, r, g)
+
+    def up(d, cc, g, device=None):
+        r = row(z - d, y, cc)
+        i = cc * PHASES + g
+        return remote(
+            source(d, cc, r, g), cut(q_all, r, g), send_up.at[d, i], recv_up.at[d, i],
+            at(z + 1, y, c) if device is None else device,
+        )
+
+    def dn(d, cc, g, device=None):
+        r = row(z + d, y, cc)
+        i = cc * PHASES + g
+        return remote(
+            source(d, cc, r, g), cut(q_all, r, g), send_dn.at[d, i], recv_dn.at[d, i],
+            at(z - 1, y, c) if device is None else device,
+        )
+
+    def across(zs, cc, g, own=False):
+        r = row(zs, y, cc)
+        i = cc * PHASES + g
+        return remote(
+            source(0 if own else 1, cc, r, g), cut(q_all, r, g),
+            send_y.at[zs, i], recv_y.at[zs, i], at(z, 1 - y, c),
+        )
+
+    def arrived(ref, r, g, send, recv):
+        remote(cut(q_all, r, g), cut(q_all, r, g), send, recv, sibling).wait_recv()
+
     meta_copies = []
-    for d in range(1, Z * Y):
-        copy = remote(
-            meta, metas.at[chip], meta_send.at[d], meta_recv.at[d],
-            {"wide": lax.rem(chip + d, Z * Y) * C + c},
-        )
-        copy.start()
-        meta_copies.append(copy)
-    copy = remote(meta, metas.at[Z * Y], meta_send.at[0], meta_recv.at[0], sibling)
-    copy.start()
-    meta_copies.append(copy)
-
-    def up(d, cc):
-        r = row(z - d, y, cc)
-        src = q_own.at[c] if d == 0 and cc == 0 else q_all.at[r]
-        return remote(src, q_all.at[r], send_up.at[d, cc], recv_up.at[d, cc], at(z + 1, y, c))
-
-    def dn(d, cc):
-        r = row(z + d, y, cc)
-        src = q_own.at[c] if d == 0 and cc == 0 else q_all.at[r]
-        return remote(src, q_all.at[r], send_dn.at[d, cc], recv_dn.at[d, cc], at(z - 1, y, c))
-
-    def across(zs, cc, own=False):
-        r = row(zs, y, cc)
-        src = q_own.at[c] if own and cc == 0 else q_all.at[r]
-        return remote(src, q_all.at[r], send_y.at[zs, cc], recv_y.at[zs, cc], at(z, 1 - y, c))
-
-    key_copy = remote(blocks, sib, one_send.at[1], one_recv.at[1], sibling)
-    for cc in range(2):
+    for d in range(1, chips):
+        meta_copies.append(
+            remote(
+                meta, metas.at[chip], meta_send.at[d], meta_recv.at[d],
+                {"wide": lax.rem(chip + d, chips) * C + c},
+            )
+        )
+    meta_copies.append(remote(meta, metas.at[chips], meta_send.at[0], meta_recv.at[0], sibling))
+    key_copy = remote(blocks, theirs, key_send, key_recv, sibling)
+
+    def send_own(cc, g):
         if cc == 1:
-            to_sib.wait_recv()
-        pl.when(z < Z - 1)(lambda: up(0, cc).start())
-        pl.when(z > 0)(lambda: dn(0, cc).start())
-        across(z, cc, True).start()
-    key_copy.start()
-    for d in range(1, Z):
+            to_sib(g).wait_recv()
+        pl.when(z < Z - 1)(lambda: up(0, cc, g).start())
+        pl.when(z > 0)(lambda: dn(0, cc, g).start())
+        across(z, cc, g, True).start()
+
+    def forward(d, g):
         for cc in range(2):
+            i = cc * PHASES + g
 
             @pl.when(z - d >= 0)
             def _():
                 r = row(z - d, y, cc)
-                remote(
-                    q_all.at[r], q_all.at[r], send_up.at[d - 1, cc], recv_up.at[d - 1, cc], sibling
-                ).wait_recv()
+                arrived(q_all, r, g, send_up.at[d - 1, i], recv_up.at[d - 1, i])
                 if d < Z - 1:
-                    pl.when(z < Z - 1)(lambda: up(d, cc).start())
-                across(z - d, cc).start()
+                    pl.when(z < Z - 1)(lambda: up(d, cc, g).start())
+                across(z - d, cc, g).start()
 
             @pl.when(z + d < Z)
             def _():
                 r = row(z + d, y, cc)
-                remote(
-                    q_all.at[r], q_all.at[r], send_dn.at[d - 1, cc], recv_dn.at[d - 1, cc], sibling
-                ).wait_recv()
+                arrived(q_all, r, g, send_dn.at[d - 1, i], recv_dn.at[d - 1, i])
                 if d < Z - 1:
-                    pl.when(z > 0)(lambda: dn(d, cc).start())
-                across(z + d, cc).start()
-
-    for zs in range(Z):
-        for cc in range(2):
-            r = row(zs, 1 - y, cc)
-            remote(
-                q_all.at[r], q_all.at[r], send_y.at[zs, cc], recv_y.at[zs, cc], sibling
-            ).wait_recv()
-            across(zs, cc).wait_send()
-    for d in range(Z - 1):
-        for cc in range(2):
-            pl.when((z - d >= 0) & (z < Z - 1))(lambda: up(d, cc).wait_send())
-            pl.when((z + d < Z) & (z > 0))(lambda: dn(d, cc).wait_send())
-    to_sib.wait_send()
-    key_copy.wait()
-    own_local.wait()
+                    pl.when(z > 0)(lambda: dn(d, cc, g).start())
+                across(z + d, cc, g).start()
+
+    def arrive_y(g):
+        for zs in range(Z):
+            for cc in range(2):
+                i = cc * PHASES + g
+                arrived(q_all, row(zs, 1 - y, cc), g, send_y.at[zs, i], recv_y.at[zs, i])
+
+    for g in range(PHASES):
+        to_sib(g).start()
+    for copy in meta_copies:
+        copy.start()
+    send_own(0, 0)
+    send_own(1, 0)
+    key_copy.start()
+    for g in range(1, PHASES):
+        send_own(0, g)
+        send_own(1, g)
+    forward(1, 0)
+    forward(2, 0)
+    forward(3, 0)
+
+    keys[:, 8 * tok :] = fresh_ref[...]
+    lane = lax.broadcasted_iota(jnp.int32, (1, tok), 1)
+    count = groups * per
+    lane_all = lax.broadcasted_iota(jnp.int32, (count, tok), 1)
+    step_of = (lax.broadcasted_iota(jnp.int32, (count, tok), 0) % per) // heads
     meta_local.wait()
     for copy in meta_copies:
-        copy.wait()
-
-
-def attention_kernel(scale, steps, heads, table, limits, where, q_ref, *refs):
-    mine, theirs = refs[:8], refs[8:16]
-    fresh_ref, o_ref, m_ref, keys = refs[16:]
-    step = pl.program_id(0)
-    tok = mine[0].shape[2]
-    groups = q_ref.shape[0]
-    per = steps * heads
-    rows = groups * per
-    latent = o_ref.shape[2]
-    q_pair = q_ref[...].astype(jnp.float32)
-    keys[:, 8 * tok :] = fresh_ref[...]
-    outs, maxes = [], []
-    lane = lax.broadcasted_iota(jnp.int32, (1, tok), 1)
-    lane_all = lax.broadcasted_iota(jnp.int32, (rows, tok), 1)
-    step_of = (lax.broadcasted_iota(jnp.int32, (rows, tok), 0) % per) // heads
-    for u in range(2):
-        k = step * 2 + u
-        query = q_pair[:, u * per : (u + 1) * per].reshape(rows, -1).astype(jnp.bfloat16)
-        for s in range(4):
-            keys[:, s * tok : (s + 1) * tok] = mine[u * 4 + s][0]
-            keys[:, (4 + s) * tok : (5 + s) * tok] = theirs[u * 4 + s][0]
-        scores = (
-            jnp.dot(query, keys[...], preferred_element_type=jnp.float32)
-            * scale
-        )
+        copy.wait_recv()
+    tag_copy = pltpu.make_async_copy(metas, tags, local_sem.at[3])
+    tag_copy.start()
+    tag_copy.wait()
+    load.wait()
+    key_copy.wait_recv()
+    own_local.wait()
+
+    def attend(g, u):
+        k = g * 2 + u
+        query = q_all[:, g * piece : (g + 1) * piece].astype(jnp.float32)
+        query = query[:, u * per : (u + 1) * per].reshape(count, -1).astype(jnp.bfloat16)
+        length = tags[k, 1, 0]
+        limits = []
+        half = tags.shape[2] // 2
+        for side, (held, tag) in enumerate(((mine, chip), (theirs, chips))):
+            for s in range(4):
+                spot = (k * C + c) * 4 + s
+                index = tags[tag, 0, spot]
+                position = tags[tag, 0, half + spot]
+                limits.append(jnp.where(position > 0, length - (position - 1) * tok, 0))
+                at_col = (side * 4 + s) * tok
+                keys[:, at_col : at_col + tok] = held[index]
+        scores = jnp.dot(query, keys[...], preferred_element_type=jnp.float32) * scale
         parts = []
         for s in range(8):
-            live = lane < limits[s // 4, k, s % 4]
-            parts.append(jnp.where(live, scores[:, s * tok : (s + 1) * tok], LOW))
-        bound = jnp.where(k == where[0], step_of, -1)
+            parts.append(jnp.where(lane < limits[s], scores[:, s * tok : (s + 1) * tok], LOW))
+        bound = jnp.where(k == chip, step_of, -1)
         parts.append(jnp.where(lane_all <= bound, scores[:, 8 * tok :], LOW))
         masked = jnp.concatenate(parts, axis=1)
         top = jnp.maximum(jnp.max(masked, axis=1, keepdims=True), -1e29)
@@ -181,11 +215,37 @@
             (((1,), (1,)), ((), ())),
             preferred_element_type=jnp.float32,
         )
-        outs.append(out.reshape(groups, per, latent))
         stat = jnp.where(lane_all == 0, top, total)
-        maxes.append(stat.reshape(groups, per, tok))
-    o_ref[...] = jnp.concatenate(outs, axis=1).astype(jnp.bfloat16)
-    m_ref[...] = jnp.concatenate(maxes, axis=1)
+        return out.reshape(groups, per, latent), stat.reshape(groups, per, tok)
+
+    def put(g, first, second):
+        span = slice(g * piece, (g + 1) * piece)
+        o_ref[:, span] = jnp.concatenate([first[0], second[0]], axis=1).astype(jnp.bfloat16)
+        m_ref[:, span] = jnp.concatenate([first[1], second[1]], axis=1)
+
+    for g in range(PHASES):
+        if g + 1 < PHASES:
+            forward(1, g + 1)
+        arrive_y(g)
+        first = attend(g, 0)
+        if g + 1 < PHASES:
+            forward(2, g + 1)
+        second = attend(g, 1)
+        if g + 1 < PHASES:
+            forward(3, g + 1)
+        put(g, first, second)
+
+    for g in range(PHASES):
+        to_sib(g).wait_send()
+        for cc in range(2):
+            for zs in range(Z):
+                across(zs, cc, g).wait_send()
+            for d in range(Z - 1):
+                pl.when((z - d >= 0) & (z < Z - 1))(lambda: up(d, cc, g).wait_send())
+                pl.when((z + d < Z) & (z > 0))(lambda: dn(d, cc, g).wait_send())
+    key_copy.wait_send()
+    for copy in meta_copies:
+        copy.wait_send()
 
 
 def reduce_kernel(
@@ -422,67 +482,33 @@
     anywhere = pl.BlockSpec(memory_space=pl.ANY)
     vmem = pl.BlockSpec(memory_space=pltpu.VMEM)
     dma = pltpu.SemaphoreType.DMA
-    q_all, sib, metas = pl.pallas_call(
-        gather_kernel,
-        out_shape=(
-            jax.ShapeDtypeStruct((members, rows, width), jnp.bfloat16),
-            jax.ShapeDtypeStruct(blocks_t.shape, jnp.bfloat16),
-            jax.ShapeDtypeStruct((half + 1,) + meta.shape, jnp.int32),
-        ),
-        in_specs=[anywhere] * 3,
-        out_specs=(anywhere,) * 3,
-        scratch_shapes=[
-            dma((2,)),
-            dma((Z, 2)), dma((Z, 2)), dma((Z, 2)),
-            dma((Z, 2)), dma((Z, 2)), dma((Z, 2)),
-            dma((2,)), dma((2,)), dma((half,)), dma((half,)),
-        ],
-        compiler_params=pltpu.CompilerParams(collective_id=0, has_side_effects=True),
-        name="gather_queries",
-    )(q_own, blocks_t, meta)
-
-    def my_side(tag_row):
-        both = tag_row[0].reshape(2, half, C, per_peer)
-        return jnp.where(c == 0, both[:, :, 0], both[:, :, 1])
-
-    mine, theirs = my_side(meta), my_side(metas[half])
-    table = jnp.stack([mine[0], theirs[0]])
-    spots = jnp.stack([mine[1], theirs[1]])
-    lengths = metas[:half, 1, 0]
-    limits = jnp.where(spots > 0, lengths[None, :, None] - (spots - 1) * tok, 0)
     fresh = jnp.zeros((width, tok), jnp.bfloat16).at[:, :steps].set(new_latent[0].T)
-
-    def key_spec(side, u, s):
-        return pl.BlockSpec(
-            (1, width, tok), lambda g, table, limits, where: (table[side, 2 * g + u, s], 0, 0)
-        )
-
-    pairs = [(u, s) for u in range(2) for s in range(per_peer)]
+    pieces = 2 * PHASES
     partial, stat = pl.pallas_call(
-        functools.partial(attention_kernel, scale, steps, heads),
+        functools.partial(attend_kernel, scale, steps, heads),
         out_shape=(
             jax.ShapeDtypeStruct((members, rows, latent), jnp.bfloat16),
             jax.ShapeDtypeStruct((members, rows, tok), jnp.float32),
         ),
-        grid_spec=pltpu.PrefetchScalarGridSpec(
-            num_scalar_prefetch=3,
-            grid=(half // 2,),
-            in_specs=[pl.BlockSpec((members, 2 * per, width), lambda g, *_: (0, g, 0))]
-            + [key_spec(0, u, s) for u, s in pairs]
-            + [key_spec(1, u, s) for u, s in pairs]
-            + [pl.BlockSpec((width, tok), lambda g, *_: (0, 0))],
-            out_specs=(
-                pl.BlockSpec((members, 2 * per, latent), lambda g, *_: (0, g, 0)),
-                pl.BlockSpec((members, 2 * per, tok), lambda g, *_: (0, g, 0)),
-            ),
-            scratch_shapes=[pltpu.VMEM((width, (2 * per_peer + 1) * tok), jnp.bfloat16)],
+        in_specs=[anywhere, anywhere, anywhere, vmem],
+        out_specs=(vmem, vmem),
+        scratch_shapes=[
+            pltpu.VMEM((members, rows, width), jnp.bfloat16),
+            pltpu.VMEM(blocks_t.shape, jnp.bfloat16),
+            pltpu.VMEM(blocks_t.shape, jnp.bfloat16),
+            pltpu.VMEM((half + 1,) + meta.shape, jnp.int32),
+            pltpu.SMEM((half + 1,) + meta.shape, jnp.int32),
+            pltpu.VMEM((width, (2 * per_peer + 1) * tok), jnp.bfloat16),
+            dma((4,)),
+            dma((Z, pieces)), dma((Z, pieces)), dma((Z, pieces)),
+            dma((Z, pieces)), dma((Z, pieces)), dma((Z, pieces)),
+            dma((PHASES,)), dma((PHASES,)), dma, dma, dma((half,)), dma((half,)),
+        ],
+        compiler_params=pltpu.CompilerParams(
+            collective_id=0, has_side_effects=True, vmem_limit_bytes=56 * MIB
         ),
-        compiler_params=pltpu.CompilerParams(vmem_limit_bytes=48 * MIB),
-        name="partial_attention",
-    )(
-        table, limits, chip.reshape(1), q_all,
-        *([blocks_t] * len(pairs)), *([sib] * len(pairs)), fresh,
-    )
+        name="gather_and_attend",
+    )(q_own, blocks_t, meta, fresh)
     stat_rows = stat[:, :, :2].transpose(2, 0, 1)
 
     chunk = (C, rows, latent)

time: 168 us -> 154 us (0.917)
  Pallas kernels: 149 us -> 141 us
  local copies, waits for them, and re-layouts: 11.8 us -> 8.25 us
    pallas_call x2 -> x1, Pallas kernels: 70.7 us -> 62.7 us  [move_queries(): pl.pallas_call(functools.partial(attend_kernel, scale, steps, heads), out...]
    slice x4 -> x0, local copies, waits for them, and re-layouts: 1.7 us -> none  [the longest x1 0.99 us: move_queries(): lengths = metas[:half, 1, 0]]
    unnamed x7 -> x4, local copies, waits for them, and re-layouts: 3.45 us -> 1.78 us
where the time goes in v3:
time: 154 us
  Pallas kernels  141 us (92%)
  local copies, waits for them, and re-layouts  8.25 us (5%)
  other arithmetic  3.25 us (2%)
    pallas_call x1, Pallas kernels, move_queries(): pl.pallas_call(functools.partial(reduce_kernel, steps, heads), out_shape=...  78 us
    pallas_call x1, Pallas kernels, move_queries(): pl.pallas_call(functools.partial(attend_kernel, scale, steps, heads), out...  62.7 us

profile of v3, /device:TPU:0, one launch (start us, length us, event | category | flops | bytes accessed | tf_op | source)
XLA Modules:
  0.0 154.1 jit_solution(1468189429760805691)
XLA Ops:
  0.0 0.0 copy-start
  0.0 0.7 compare_reduce_fusion
  1.4 0.9 convert_reduce_fusion
  2.3 0.7 compare_select_fusion
  3.0 0.1 select_reduce_fusion.1
  3.1 0.1 add_bitcast_fusion
  3.2 0.6 concatenate.13.meta
  3.8 0.9 copy.23
  4.7 0.9 copy.26
  5.6 0.7 select_bitcast_fusion
  6.3 0.7 scatter.4.fresh_ref
  7.0 0.0 copy-done
  7.0 1.2 fusion
  8.2 0.1 copy.24
  8.3 0.8 copy.25
  9.1 62.7 %gather_and_attend.1 = (bf16[16,192,512]{2,1,0:T(8,128)(2,1)}, f32[16,192,128]{2,1,0:T(8,128)}) custom-call(bf16[2,192,576]{2,1,0:T(8,128)(2,1)} %bitcast.27, bf16[64,576,128]{2,1,0:T(8,128)(2,1)} %bitcast.26, s32[8,128]{1,0:T(8,128)} %concatenate.13.meta, bf16[576,128]{1,0:T(8,128)(2,1)} %scatter.4.fresh_ref), custom_call_target="tpu_custom_call" | custom-call | tf_op jit(solution)/shard_map/gather_and_attend/pallas_call | solution.py:487
  71.9 2.1 %copy.27 = f32[16,192,128]{1,0,2:T(8,128)S(1)} copy(f32[16,192,128]{2,1,0:T(8,128)} %get-tuple-element.20) | data formatting | bytes 3145728 | tf_op jit(solution)/shard_map/gather_and_attend/pallas_call | solution.py:487
  74.0 0.6 slice_bitcast_fusion.stat_ref
  74.7 78.0 %reduce_partials.1 = bf16[48,512]{1,0:T(8,128)(2,1)} custom-call(bf16[16,192,512]{2,1,0:T(8,128)(2,1)} %get-tuple-element.19.o_ref, f32[2,16,192]{2,1,0:T(8,128)} %slice_bitcast_fusion.stat_ref, bf16[8,512,128]{2,1,0:T(8,128)(2,1)} %w_uv_ref.1, bf16[1024,7168]{1,0:T(8,128)(2,1)} %w_o_ref.1), custom_call_target="tpu_custom_call" | custom-call | tf_op jit(solution)/shard_map/reduce_partials/pallas_call | solution.py:519
  152.6 1.5 reshape.52
  (1 shorter events, 0.0 us)
Async XLA Ops:
  0.0 7.0 %copy-start = (bf16[8,128,512]{2,1,0:T(8,128)(2,1)S(1)}, bf16[8,128,512]{2,1,0:T(8,128)(2,1)}, u32[]{:S(2)}) copy-start(bf16[8,128,512]{2,1,0:T(8,128)(2,1)} %param.18) | copy-start | bytes 3145732

commit v4 on v3

--- a/solution.py
+++ b/solution.py
@@ -286,98 +286,110 @@
 
     f_all = square_t[:width, :groups]
 
-    def scale_chunk(base):
+    piece = width // PHASES
+
+    def span(g):
+        return pl.ds(g * piece, piece)
+
+    def scale_chunk(base, g):
+        f_rows = f_all[g * piece : (g + 1) * piece]
+        lanes = lax.broadcasted_iota(jnp.int32, f_rows.shape, 1)
         for cc in range(C):
             j = base + cc
-            lanes = lax.broadcasted_iota(jnp.int32, f_all.shape, 1)
-            factor = jnp.sum(jnp.where(lanes == j, f_all, 0.0), axis=1, keepdims=True)
-            scaled[j] = (o_ref[j].astype(jnp.float32) * factor).astype(jnp.bfloat16)
+            factor = jnp.sum(jnp.where(lanes == j, f_rows, 0.0), axis=1, keepdims=True)
+            scaled[j, span(g)] = (o_ref[j, span(g)].astype(jnp.float32) * factor).astype(
+                jnp.bfloat16
+            )
 
     order = (3, 0, 2, 1)
 
-    def y_copy(t):
+    def y_copy(t, g):
         base = (t * Y + 1 - y) * C
         return remote(
-            scaled.at[pl.ds(base, C)], y_in.at[t], send_y.at[t], recv_y.at[t], at(z, 1 - y, c)
-        )
-
-    for t in order:
-        scale_chunk((t * Y + 1 - y) * C)
-        y_copy(t).start()
-    for t in order:
-        scale_chunk((t * Y + y) * C)
-
-    def up_copy(t):
-        return remote(
-            up_out.at[t], up_in.at[t], send_up.at[t], recv_up.at[t], at(z + 1, y, c)
-        )
-
-    def dn_copy(t):
-        return remote(
-            dn_out.at[t], dn_in.at[t], send_dn.at[t], recv_dn.at[t], at(z - 1, y, c)
-        )
-
-    def up_arrived(t):
-        remote(
-            up_out.at[t], up_in.at[t], send_up.at[t], recv_up.at[t], at(z, y, 1 - c)
-        ).wait_recv()
-
-    def dn_arrived(t):
-        remote(
-            dn_out.at[t], dn_in.at[t], send_dn.at[t], recv_dn.at[t], at(z, y, 1 - c)
-        ).wait_recv()
-
-    def get_y(t):
-        y_copy(t).wait_recv()
-        mine = scaled[pl.ds((t * Y + y) * C, C)].astype(jnp.float32)
-        acc[t] = mine + y_in[t].astype(jnp.float32)
-
-    def send_upward(t):
+            scaled.at[pl.ds(base, C), span(g)], y_in.at[t, :, span(g)],
+            send_y.at[t, g], recv_y.at[t, g], at(z, 1 - y, c),
+        )
+
+    for g in range(PHASES):
+        for t in order:
+            scale_chunk((t * Y + 1 - y) * C, g)
+            y_copy(t, g).start()
+    for g in range(PHASES):
+        for t in order:
+            scale_chunk((t * Y + y) * C, g)
+
+    def up_copy(t, g, device=None):
+        return remote(
+            up_out.at[t, :, span(g)], up_in.at[t, :, span(g)], send_up.at[t, g], recv_up.at[t, g],
+            at(z + 1, y, c) if device is None else device,
+        )
+
+    def dn_copy(t, g, device=None):
+        return remote(
+            dn_out.at[t, :, span(g)], dn_in.at[t, :, span(g)], send_dn.at[t, g], recv_dn.at[t, g],
+            at(z - 1, y, c) if device is None else device,
+        )
+
+    near = at(z, y, 1 - c)
+
+    def get_y(t, g):
+        y_copy(t, g).wait_recv()
+        mine = scaled[pl.ds((t * Y + y) * C, C), span(g)].astype(jnp.float32)
+        acc[t, :, span(g)] = mine + y_in[t, :, span(g)].astype(jnp.float32)
+
+    def send_upward(t, g):
         @pl.when(z == 0)
         def _():
-            up_out[t] = acc[t].astype(jnp.bfloat16)
+            up_out[t, :, span(g)] = acc[t, :, span(g)].astype(jnp.bfloat16)
 
         @pl.when((z > 0) & (z < t))
         def _():
-            up_arrived(t)
-            up_out[t] = (acc[t] + up_in[t].astype(jnp.float32)).astype(jnp.bfloat16)
-
-        pl.when(z < t)(lambda: up_copy(t).start())
-
-    def send_downward(t):
+            up_copy(t, g, near).wait_recv()
+            total = acc[t, :, span(g)] + up_in[t, :, span(g)].astype(jnp.float32)
+            up_out[t, :, span(g)] = total.astype(jnp.bfloat16)
+
+        pl.when(z < t)(lambda: up_copy(t, g).start())
+
+    def send_downward(t, g):
         @pl.when(z == Z - 1)
         def _():
-            dn_out[t] = acc[t].astype(jnp.bfloat16)
+            dn_out[t, :, span(g)] = acc[t, :, span(g)].astype(jnp.bfloat16)
 
         @pl.when((z < Z - 1) & (z > t))
         def _():
-            dn_arrived(t)
-            dn_out[t] = (acc[t] + dn_in[t].astype(jnp.float32)).astype(jnp.bfloat16)
-
-        pl.when(z > t)(lambda: dn_copy(t).start())
-
-    get_y(3)
-    send_upward(3)
-    get_y(0)
-    send_downward(0)
-    get_y(2)
-    send_upward(2)
-    get_y(1)
-    send_downward(1)
-    send_upward(1)
-    send_downward(2)
-    for t in range(Z):
-
-        @pl.when(z == t)
-        def _():
-            value = acc[t]
-            if t > 0:
-                up_arrived(t)
-                value = value + up_in[t].astype(jnp.float32)
-            if t < Z - 1:
-                dn_arrived(t)
-                value = value + dn_in[t].astype(jnp.float32)
-            fin[...] = value.astype(jnp.bfloat16)
+            dn_copy(t, g, near).wait_recv()
+            total = acc[t, :, span(g)] + dn_in[t, :, span(g)].astype(jnp.float32)
+            dn_out[t, :, span(g)] = total.astype(jnp.bfloat16)
+
+        pl.when(z > t)(lambda: dn_copy(t, g).start())
+
+    def by_half(low, high):
+        pl.when(z < Z // 2)(low)
+        pl.when(z >= Z // 2)(high)
+
+    for g in range(PHASES):
+        get_y(3, g)
+        get_y(0, g)
+        by_half(lambda: send_upward(3, g), lambda: send_downward(0, g))
+        get_y(2, g)
+        pl.when(z < Z // 2)(lambda: send_upward(2, g))
+        get_y(1, g)
+        by_half(lambda: send_upward(1, g), lambda: send_downward(1, g))
+        pl.when(z >= Z // 2)(lambda: send_downward(2, g))
+        by_half(lambda: send_downward(0, g), lambda: send_upward(3, g))
+    for g in range(PHASES):
+        for t in range(Z):
+
+            @pl.when(z == t)
+            def _():
+                value = acc[t, :, span(g)]
+                if t > 0:
+                    up_copy(t, g, near).wait_recv()
+                    value = value + up_in[t, :, span(g)].astype(jnp.float32)
+                if t < Z - 1:
+                    dn_copy(t, g, near).wait_recv()
+                    value = value + dn_in[t, :, span(g)].astype(jnp.float32)
+                fin[:, span(g)] = value.astype(jnp.bfloat16)
 
     swap = remote(fin.at[1 - c], sib_in, sib_send, sib_recv, at(z, y, 1 - c))
     swap.start()
@@ -434,9 +446,10 @@
     for copy in row_copies:
         copy.wait_send()
     for t in range(Z):
-        y_copy(t).wait_send()
-        pl.when(z < t)(lambda: up_copy(t).wait_send())
-        pl.when(z > t)(lambda: dn_copy(t).wait_send())
+        for g in range(PHASES):
+            y_copy(t, g).wait_send()
+            pl.when(z < t)(lambda: up_copy(t, g).wait_send())
+            pl.when(z > t)(lambda: dn_copy(t, g).wait_send())
     for copy in stat_copies:
         copy.wait_send()
 
@@ -540,7 +553,7 @@
             pltpu.VMEM((half, tall, tile), jnp.bfloat16),
             pltpu.VMEM((half - 1, tall, tile), jnp.bfloat16),
             dma((half,)), dma((half,)),
-            dma((Z,)), dma((Z,)), dma((Z,)), dma((Z,)), dma((Z,)), dma((Z,)),
+            *([dma((Z, PHASES))] * 6),
             dma, dma,
             dma, dma((tiles,)), dma((tiles,)), dma((half,)), dma((half,)),
         ],

time: 154 us -> 147 us (0.955)
  Pallas kernels: 141 us -> 133 us
    pallas_call x1, Pallas kernels: 78 us -> 70.5 us  [move_queries(): pl.pallas_call(functools.partial(reduce_kernel, steps, heads), out_shape=...]
where the time goes in v4:
time: 147 us
  Pallas kernels  133 us (90%)
  local copies, waits for them, and re-layouts  8.25 us (6%)
  other arithmetic  3.25 us (2%)
    pallas_call x1, Pallas kernels, move_queries(): pl.pallas_call(functools.partial(reduce_kernel, steps, heads), out_shape=...  70.5 us
    pallas_call x1, Pallas kernels, move_queries(): pl.pallas_call(functools.partial(attend_kernel, scale, steps, heads), out...  62.7 us

profile of v4, /device:TPU:0, one launch (start us, length us, event | category | flops | bytes accessed | tf_op | source)
XLA Modules:
  0.0 146.6 jit_solution(2436991156572938363)
XLA Ops:
  0.0 0.0 copy-start
  0.0 0.7 compare_reduce_fusion
  1.4 0.9 convert_reduce_fusion
  2.3 0.7 compare_select_fusion
  3.0 0.1 select_reduce_fusion.1
  3.1 0.1 add_bitcast_fusion
  3.2 0.6 concatenate.13.meta
  3.8 0.9 copy.23
  4.7 0.9 copy.26
  5.6 0.7 select_bitcast_fusion
  6.3 0.7 scatter.4.fresh_ref
  7.0 0.0 copy-done
  7.0 1.2 fusion
  8.2 0.1 copy.24
  8.3 0.8 copy.25
  9.1 62.7 %gather_and_attend.1 = (bf16[16,192,512]{2,1,0:T(8,128)(2,1)}, f32[16,192,128]{2,1,0:T(8,128)}) custom-call(bf16[2,192,576]{2,1,0:T(8,128)(2,1)} %bitcast.27, bf16[64,576,128]{2,1,0:T(8,128)(2,1)} %bitcast.26, s32[8,128]{1,0:T(8,128)} %concatenate.13.meta, bf16[576,128]{1,0:T(8,128)(2,1)} %scatter.4.fresh_ref), custom_call_target="tpu_custom_call" | custom-call | tf_op jit(solution)/shard_map/gather_and_attend/pallas_call | solution.py:500
  71.9 2.1 %copy.27 = f32[16,192,128]{1,0,2:T(8,128)S(1)} copy(f32[16,192,128]{2,1,0:T(8,128)} %get-tuple-element.20) | data formatting | bytes 3145728 | tf_op jit(solution)/shard_map/gather_and_attend/pallas_call | solution.py:500
  74.0 0.6 slice_bitcast_fusion.stat_ref
  74.7 70.5 %reduce_partials.1 = bf16[48,512]{1,0:T(8,128)(2,1)} custom-call(bf16[16,192,512]{2,1,0:T(8,128)(2,1)} %get-tuple-element.19.o_ref, f32[2,16,192]{2,1,0:T(8,128)} %slice_bitcast_fusion.stat_ref, bf16[8,512,128]{2,1,0:T(8,128)(2,1)} %w_uv_ref.1, bf16[1024,7168]{1,0:T(8,128)(2,1)} %w_o_ref.1), custom_call_target="tpu_custom_call" | custom-call | tf_op jit(solution)/shard_map/reduce_partials/pallas_call | solution.py:532
  145.2 1.5 reshape.52
  (1 shorter events, 0.0 us)
Async XLA Ops:
  0.0 7.0 %copy-start = (bf16[8,128,512]{2,1,0:T(8,128)(2,1)S(1)}, bf16[8,128,512]{2,1,0:T(8,128)(2,1)}, u32[]{:S(2)}) copy-start(bf16[8,128,512]{2,1,0:T(8,128)(2,1)} %param.18) | copy-start | bytes 3145732
